TPU v7x, 256 devices: a whole 4x4x8 slice. The times are simulated.
256 devices in a mesh: dp: 16 (over y, x), tensor: 16 (over z, core).
Axes of the slice: x: 4, y: 4, z: 8, core: 2. Of those that a mesh axis runs over, the one named last changes fastest.
Arguments:
- buffer: bfloat16 [26624, 16384], P('dp', 'tensor'), may hold values from -1700 to 1700
- old_basis: bfloat16 [16384, 1024], P('tensor', 'dp'), may hold values from -0.046875 to 0.046875
Outputs:
- new_buffer: bfloat16 [26624, 16384], P('dp', 'tensor')
- weight_update: bfloat16 [26624, 16384], P('dp', 'tensor')
- new_basis: bfloat16 [16384, 1024], P('tensor', 'dp')
All inputs are finite; a program needn't handle non-finite values.
Results may differ from a plain program's by a relative error of at most 0.015.
Values may be sent and summed in bfloat16 or wider, within the bound.
A program may use at most 128 MiB of HBM per device.

v0:
```python
import math

import jax
import jax.numpy as jnp
from jax import lax
from jax.sharding import PartitionSpec as P

NORM_EPS = 1e-06
FEEDBACK_SHARE = 0.05


def body(buffer, old_basis):
    full_basis = lax.all_gather(old_basis, "dp", axis=1, tiled=True)
    groups = lax.axis_size("tensor")
    projected = lax.psum_scatter(
        jnp.dot(buffer, full_basis, preferred_element_type=jnp.float32),
        "tensor",
        scatter_dimension=0,
        tiled=True,
    )
    gram_part = lax.dot_general(
        projected,
        projected,
        (((0,), (0,)), ((), ())),
        precision=lax.Precision.HIGHEST,
        preferred_element_type=jnp.float32,
    )
    gram_whole = lax.psum(gram_part, ("dp", "tensor"))
    factor_low = jnp.linalg.cholesky(gram_whole)
    orthonormal = jax.scipy.linalg.solve_triangular(factor_low, projected.T, lower=True).T
    ortho_half = orthonormal.astype(jnp.bfloat16)
    ortho_all = lax.all_gather(ortho_half, "tensor", axis=0, tiled=True)
    trans_part = lax.dot_general(
        buffer, ortho_all, (((0,), (0,)), ((), ())), preferred_element_type=jnp.float32
    )
    rank_full = full_basis.shape[1]
    shares = lax.psum_scatter(trans_part, "dp", scatter_dimension=1, tiled=True)
    totals = lax.psum(jnp.sum(shares * shares, axis=0), "tensor")
    trans_half = shares.astype(jnp.bfloat16)
    new_basis = (trans_half.astype(jnp.float32) * lax.rsqrt(totals + NORM_EPS)).astype(jnp.bfloat16)
    trans_all, basis_all = (
        lax.all_gather(trans_half, "dp", axis=1, tiled=True),
        lax.all_gather(new_basis, "dp", axis=1, tiled=True),
    )
    feedback = lax.dot_general(
        ortho_all, trans_all, (((1,), (1,)), ((), ())), preferred_element_type=jnp.float32
    )
    new_buffer = (buffer.astype(jnp.float32) - FEEDBACK_SHARE * feedback).astype(jnp.bfloat16)
    scale_up = math.sqrt(
        buffer.shape[0] * lax.axis_size("dp") * buffer.shape[1] * groups / rank_full
    )
    product = lax.dot_general(
        ortho_all, basis_all, (((1,), (1,)), ((), ())), preferred_element_type=jnp.float32
    )
    weight_update = (-scale_up * product).astype(jnp.bfloat16)
    return (new_buffer, weight_update, new_basis)


def solution(mesh):
    in_specs = (P("dp", "tensor"), P("tensor", "dp"))
    out_specs = (P("dp", "tensor"), P("dp", "tensor"), P("tensor", "dp"))
    return jax.shard_map(body, mesh=mesh, in_specs=in_specs, out_specs=out_specs, check_vma=False)
```

profile of v0, /device:TPU:1, one launch (start us, length us, event | category | flops | bytes accessed | tf_op | source)
XLA Modules:
  0.0 1022.8 jit_solution(10015789408386284110)
XLA Ops:
  7.9 55.4 %all-gather.5.cloned.1.call-done = bf16[1024,1024]{0,1:T(8,128)(2,1)} async-done(((bf16[1024,64]{0,1:T(8,128)(2,1)}), bf16[1024,1024]{0,1:T(8,128)(2,1)}) %all-gather.5.cloned.1.call-update) | async-done | bytes 2097168 | tf_op jit(solution)/shard_map/all_gather | solution.py:13
  63.4 9.2 fusion.63
  72.6 64.9 %reduce-scatter.3.cloned.1.call-done = f32[104,1024]{1,0:T(8,128)} async-done(((f32[1664,1024]{1,0:T(8,128)}), f32[104,1024]{1,0:T(8,128)}) %reduce-scatter.3.cloned.1.call-update) | async-done | bytes 426000 | tf_op jit(solution)/shard_map/reduce_scatter | solution.py:15
  137.5 6.6 fusion.64
  144.1 268.7 %all-reduce.3.cloned.1.call-done = f32[1024,1024]{0,1:T(8,128)} async-done(((f32[1024,1024]{0,1:T(8,128)}), f32[1024,1024]{0,1:T(8,128)}) %all-reduce.3.cloned.1.call-update) | async-done | bytes 4194320 | tf_op jit(solution)/shard_map/psum | solution.py:28
  412.8 5.8 copy.6
  418.6 4.4 fusion
  425.0 11.7 %cholesky.223 = f32[128,128]{1,0:T(8,128)S(1)} custom-call(f32[128,128]{1,0:T(8,128)S(1)} %cholesky.580), custom_call_target="Cholesky" | custom-call | tf_op jit(solution)/shard_map/jit(cholesky)/cholesky | solution.py:29
  436.8 9.8 custom-call.63
  446.6 2.5 cholesky.255
  449.1 2.4 constant_dynamic-update-slice_fusion.32
  453.0 11.9 %cholesky.244 = f32[128,128]{1,0:T(8,128)S(1)} custom-call(f32[128,128]{1,0:T(8,128)S(1)} %cholesky.584), custom_call_target="Cholesky" | custom-call | tf_op jit(solution)/shard_map/jit(cholesky)/cholesky | solution.py:29
  465.5 9.8 custom-call.64
  476.6 2.1 convolution_subtract_fusion.1
  478.7 11.7 %cholesky.468 = f32[128,128]{1,0:T(8,128)S(1)} custom-call(f32[128,128]{1,0:T(8,128)S(1)} %cholesky.589), custom_call_target="Cholesky" | custom-call | tf_op jit(solution)/shard_map/jit(cholesky)/cholesky | solution.py:29
  491.8 9.8 custom-call.65
  502.7 2.3 convolution_subtract_fusion.2
  505.1 11.9 %cholesky.487 = f32[128,128]{1,0:T(8,128)S(1)} custom-call(f32[128,128]{1,0:T(8,128)S(1)} %cholesky.594), custom_call_target="Cholesky" | custom-call | tf_op jit(solution)/shard_map/jit(cholesky)/cholesky | solution.py:29
  518.3 9.8 custom-call.66
  529.3 2.3 convolution_subtract_fusion.3
  531.6 11.7 %cholesky.506 = f32[128,128]{1,0:T(8,128)S(1)} custom-call(f32[128,128]{1,0:T(8,128)S(1)} %cholesky.599), custom_call_target="Cholesky" | custom-call | tf_op jit(solution)/shard_map/jit(cholesky)/cholesky | solution.py:29
  544.7 10.2 custom-call.67
  555.9 2.3 convolution_subtract_fusion.4
  558.2 11.7 %cholesky.526 = f32[128,128]{1,0:T(8,128)S(1)} custom-call(f32[128,128]{1,0:T(8,128)S(1)} %cholesky.604), custom_call_target="Cholesky" | custom-call | tf_op jit(solution)/shard_map/jit(cholesky)/cholesky | solution.py:29
  571.2 9.8 custom-call.68
  581.9 2.0 convolution_subtract_fusion.5
  584.0 11.9 %cholesky.546 = f32[128,128]{1,0:T(8,128)S(1)} custom-call(f32[128,128]{1,0:T(8,128)S(1)} %cholesky.609), custom_call_target="Cholesky" | custom-call | tf_op jit(solution)/shard_map/jit(cholesky)/cholesky | solution.py:29
  597.2 9.8 custom-call.69
  609.6 11.7 %cholesky.564 = f32[128,128]{1,0:T(8,128)S(1)} custom-call(f32[128,128]{1,0:T(8,128)S(1)} %convolution_subtract_fusion.6), custom_call_target="Cholesky" | custom-call | tf_op jit(solution)/shard_map/jit(cholesky)/cholesky | solution.py:29
  628.6 4.8 select_select_fusion
  633.5 23.2 %while.1 = (s32[]{:T(128)}, f32[1024,1024]{1,0:T(8,128)}, s32[8,2]{0,1:T(2,128)S(1)}, f32[8,128,128]{2,1,0:T(8,128)S(1)}, s32[]{:T(128)}) while((s32[]{:T(128)}, f32[1024,1024]{1,0:T(8,128)}, s32[8,2]{0,1:T(2,128)S(1)}, f32[8,128,128]{2,1,0:T(8,128)S(1)}, s32[]{:T(128)}) %tuple.58), condition=%wide.while_cond, body=%wide.while_body.sunk | while | flops 2 | bytes 131181 | solution.py:30
  634.1 2.3 bitcast_dynamic-update-slice_fusion.2
  637.0 2.3 bitcast_dynamic-update-slice_fusion.2
  639.9 2.3 bitcast_dynamic-update-slice_fusion.2
  642.8 2.3 bitcast_dynamic-update-slice_fusion.2
  645.7 2.3 bitcast_dynamic-update-slice_fusion.2
  648.6 2.3 bitcast_dynamic-update-slice_fusion.2
  651.5 2.3 bitcast_dynamic-update-slice_fusion.2
  654.4 2.2 bitcast_dynamic-update-slice_fusion.2
  656.7 78.8 %custom-call.70 = f32[8,128,128]{1,2,0:T(8,128)S(1)} custom-call(f32[8,128,128]{2,1,0:T(8,128)S(1)} %get-tuple-element.10), custom_call_target="InvertDiagBlocksLowerTriangular" | custom-call | tf_op jit(solution)/shard_map/jit(_solve_triangular)/triangular_solve | solution.py:30
  747.8 42.1 %all-gather.7.cloned.1.call-done = bf16[1664,1024]{1,0:T(8,128)(2,1)} async-done(((bf16[104,1024]{1,0:T(8,128)(2,1)}), bf16[1664,1024]{1,0:T(8,128)(2,1)}) %all-gather.7.cloned.1.call-update) | async-done | bytes 3407888 | tf_op jit(solution)/shard_map/all_gather | solution.py:32
  789.9 8.9 convolution_bitcast_fusion
  799.0 79.4 %reduce-scatter.5.cloned.1.call-done = f32[1024,64]{0,1:T(8,128)} async-done(((f32[1024,1024]{0,1:T(8,128)}), f32[1024,64]{0,1:T(8,128)}) %reduce-scatter.5.cloned.1.call-update) | async-done | bytes 262160 | tf_op jit(solution)/shard_map/reduce_scatter | solution.py:37
  879.4 25.7 %psum.15 = f32[64]{0:T(128)S(1)} all-reduce(f32[64]{0:T(128)S(1)} %multiply_reduce_fusion), channel_id=1, replica_groups=mesh['dp'=16,'tensor'=16] {'tensor'}, use_global_device_ids=true, to_apply=%region_20.21 | all-reduce | flops 64 | bytes 512 | tf_op jit(solution)/shard_map/psum | solution.py:38
  907.6 47.5 %all-gather.11.cloned.1.call-done = bf16[1024,1024]{0,1:T(8,128)(2,1)} async-done(((bf16[1024,64]{0,1:T(8,128)(2,1)}), bf16[1024,1024]{0,1:T(8,128)(2,1)}) %all-gather.11.cloned.1.call-update) | async-done | bytes 2097168 | tf_op jit(solution)/shard_map/all_gather | solution.py:43
  955.0 8.1 multiply_convert_fusion
  963.1 44.3 %all-gather.9.cloned.1.call-done = bf16[1024,1024]{0,1:T(8,128)(2,1)} async-done(((bf16[1024,64]{0,1:T(8,128)(2,1)}), bf16[1024,1024]{0,1:T(8,128)(2,1)}) %all-gather.9.cloned.1.call-update) | async-done | bytes 2097168 | tf_op jit(solution)/shard_map/all_gather | solution.py:42
  1007.4 8.2 subtract_convert_fusion
  (96 shorter events, 42.4 us)
Async XLA Ops:
  7.2 56.2 %all-gather.5.cloned.1.call-start = ((), (), s32[]{:S(2)}) async-start(), calls=%async_computation.2 | async-start | bytes 2228224 | tf_op jit(solution)/shard_map/all_gather | solution.py:13
  7.9 129.6 %reduce-scatter.3.cloned.1.call-start = ((), (), s32[]{:S(2)}) async-start(), calls=%async_computation.3 | async-start | bytes 7241728 | tf_op jit(solution)/shard_map/reduce_scatter | solution.py:15
  72.6 340.2 %all-reduce.3.cloned.1.call-start = ((), (), s32[]{:S(2)}) async-start(), calls=%async_computation.4 | async-start | bytes 8388608 | tf_op jit(solution)/shard_map/psum | solution.py:28
  144.1 645.9 %all-gather.7.cloned.1.call-start = ((), (), s32[]{:S(2)}) async-start(), calls=%async_computation.5 | async-start | bytes 3620864 | tf_op jit(solution)/shard_map/all_gather | solution.py:32
  423.1 1.9 copy-start
  628.6 106.9 %copy-start.1 = (f32[104,1024]{1,0:T(8,128)S(1)}, f32[104,1024]{1,0:T(8,128)}, u32[]{:S(2)}) copy-start(f32[104,1024]{1,0:T(8,128)} %reduce-scatter.3.cloned.1.call-done) | copy-start | bytes 1277956
  747.1 0.7 copy-start.2
  747.8 130.5 %reduce-scatter.5.cloned.1.call-start = ((), (), s32[]{:S(2)}) async-start(), calls=%async_computation.6 | async-start | bytes 4456448 | tf_op jit(solution)/shard_map/reduce_scatter | solution.py:37
  798.9 156.1 %all-gather.11.cloned.1.call-start = ((), (), s32[]{:S(2)}) async-start(), calls=%async_computation.8 | async-start | bytes 2228224 | tf_op jit(solution)/shard_map/all_gather | solution.py:43
  906.8 100.6 %all-gather.9.cloned.1.call-start = ((), (), s32[]{:S(2)}) async-start(), calls=%async_computation.7 | async-start | bytes 2228224 | tf_op jit(solution)/shard_map/all_gather | solution.py:42
  907.6 99.9 %copy-start.3 = (bf16[1664,1024]{1,0:T(8,128)(2,1)S(1)}, bf16[1664,1024]{1,0:T(8,128)(2,1)}, u32[]{:S(2)}) copy-start(bf16[1664,1024]{1,0:T(8,128)(2,1)} %param.2) | copy-start | bytes 10223620
Sparse Core Ops, SparseCore 0:
  10.4 52.8 all-gather.4
  72.7 64.7 reduce-scatter.2
  144.2 268.5 all-reduce.2
  747.9 41.9 all-gather.6
  799.0 79.2 reduce-scatter.4
  906.9 48.0 all-gather.10
  958.0 49.3 all-gather.8
where the time goes:
time: 1030 us; the launch traced here: 1020 us
  waiting for transfers between devices  603 us (59%)
  other arithmetic  263 us (26%)
  matrix products  75.4 us (7%)
  local copies, waits for them, and re-layouts  34.1 us (3%)
  blocking collectives  25.7 us (2%)
  between operations  20 us (2%)
    psum x1, waiting for transfers between devices, body(): gram_whole = lax.psum(gram_part, ('dp', 'tensor'))  269 us
    another operation x30, other arithmetic, body(): factor_low = jnp.linalg.cholesky(gram_whole)  173 us
    another operation x3, other arithmetic, body(): jax.scipy.linalg.solve_triangular(factor_low, projected.T, lower=True)  83.7 us
    reduce_scatter x1, waiting for transfers between devices, body(): shares = lax.psum_scatter(trans_part, 'dp', scatter_dimension=1, tiled=True)  79.4 us
    reduce_scatter x1, waiting for transfers between devices, body(): lax.psum_scatter(jnp.dot(buffer, full_basis, preferred_element_type=jnp.f...  64.9 us
    all_gather x1, waiting for transfers between devices, body(): full_basis = lax.all_gather(old_basis, 'dp', axis=1, tiled=True)  55.4 us
    all_gather x1, waiting for transfers between devices, body(): lax.all_gather(new_basis, 'dp', axis=1, tiled=True)  47.5 us
    all_gather x1, waiting for transfers between devices, body(): lax.all_gather(trans_half, 'dp', axis=1, tiled=True)  44.3 us
  transfers between devices with their start and end apart: 7, of which 7 were waited for; matrix products, arithmetic and copies ran while one was open for 1% of the time, Pallas kernels for 0%

commit v1 on v0

v1 whole, which is shorter than its diff:
```python
import math

import jax
import jax.numpy as jnp
from jax import lax
from jax.experimental import pallas as pl
from jax.experimental.pallas import tpu as pltpu
from jax.sharding import PartitionSpec as P

NORM_EPS = 1e-06
FEEDBACK_SHARE = 0.05
HI = lax.Precision.HIGHEST
F32 = jnp.float32
BF16 = jnp.bfloat16
NB = 128
MP = 16


def mm_tn(a, b, precision=None):
    return lax.dot_general(
        a, b, (((0,), (0,)), ((), ())), precision=precision, preferred_element_type=F32
    )


def mm_nn(a, b, precision=None):
    return lax.dot_general(
        a, b, (((1,), (0,)), ((), ())), precision=precision, preferred_element_type=F32
    )


def mm_nt(a, b, precision=None):
    return lax.dot_general(
        a, b, (((1,), (1,)), ((), ())), precision=precision, preferred_element_type=F32
    )


def eliminate_rows(rows, r0):
    lane = lax.broadcasted_iota(jnp.int32, (MP, NB), 1)
    row = lax.broadcasted_iota(jnp.int32, (MP, NB), 0)
    cols = [jnp.broadcast_to(rows[:, r0 + c : r0 + c + 1], (MP, NB)) for c in range(MP)]
    scale = jnp.zeros((MP, NB), F32)
    for c in range(MP):
        rs = lax.rsqrt(cols[c][c : c + 1, :])
        f = jnp.where(row > c, cols[c] * (rs * rs), 0.0)
        rows = jnp.where(lane == r0 + c, jnp.where(row == c, 1.0, 0.0), rows)
        for c2 in range(c + 1, MP):
            cols[c2] = cols[c2] - f * cols[c2][c : c + 1, :]
        rows = rows - f * rows[c : c + 1, :]
        scale = jnp.where(row == c, rs, scale)
    return rows * scale


def eliminate_block(block):
    lane = lax.broadcasted_iota(jnp.int32, (NB, NB), 1)
    for r0 in range(0, NB, MP):
        rows = eliminate_rows(block[r0 : r0 + MP, :], r0)
        block[r0 : r0 + MP, :] = rows
        if r0 + MP < NB:
            update = mm_tn(rows, rows, HI)[r0 + MP :, :]
            below = lane[r0 + MP :, :]
            old = jnp.where((below >= r0) & (below < r0 + MP), 0.0, block[r0 + MP :, :])
            block[r0 + MP :, :] = old - update


def chol_inv_kernel(g_ref, out_ref, block):
    n = g_ref.shape[0]
    nblk = n // NB
    out_ref[...] = g_ref[...]
    lane = lax.broadcasted_iota(jnp.int32, (NB, NB), 1)
    row = lax.broadcasted_iota(jnp.int32, (NB, NB), 0)

    def step(k, _):
        k0 = pl.multiple_of(k * NB, NB)
        block[...] = out_ref[pl.ds(k0, NB), pl.ds(k0, NB)]
        eliminate_block(block)
        linv = jnp.where(lane <= row, block[...], 0.0)
        out_ref[pl.ds(k0, NB), :] = mm_nn(linv, out_ref[pl.ds(k0, NB), :], HI)
        out_ref[pl.ds(k0, NB), pl.ds(k0, NB)] = linv

        def below(i, _):
            i0 = pl.multiple_of(i * NB, NB)
            u = out_ref[pl.ds(k0, NB), pl.ds(i0, NB)]
            out_ref[pl.ds(i0, NB), pl.ds(k0, NB)] = jnp.zeros((NB, NB), F32)
            out_ref[pl.ds(i0, NB), :] = out_ref[pl.ds(i0, NB), :] - mm_tn(
                u, out_ref[pl.ds(k0, NB), :], HI
            )
            return 0

        lax.fori_loop(k + 1, nblk, below, 0)
        return 0

    lax.fori_loop(0, nblk, step, 0)
    for k0 in range(0, n - NB, NB):
        out_ref[k0 : k0 + NB, k0 + NB :] = jnp.zeros((NB, n - k0 - NB), F32)


def chol_inv(g):
    n = g.shape[0]
    return pl.pallas_call(
        chol_inv_kernel,
        out_shape=jax.ShapeDtypeStruct((n, n), F32),
        in_specs=[pl.BlockSpec(memory_space=pltpu.VMEM)],
        out_specs=pl.BlockSpec(memory_space=pltpu.VMEM),
        scratch_shapes=[pltpu.VMEM((NB, NB), F32)],
        compiler_params=pltpu.CompilerParams(vmem_limit_bytes=40 << 20),
        cost_estimate=pl.CostEstimate(flops=60_000_000_000, bytes_accessed=8 << 20, transcendentals=0),
        name="chol_inv",
    )(g)


def rcopy(src, dst, send_sem, recv_sem, device):
    return pltpu.make_async_remote_copy(
        src_ref=src, dst_ref=dst, send_sem=send_sem, recv_sem=recv_sem,
        device_id=device, device_id_type=pl.DeviceIdType.MESH,
    )


def dp_steps(core):
    dp = lax.axis_index("dp")
    x, y = lax.rem(dp, 4), dp // 4

    def pairs(v):
        gray, high = lax.rem(v + v // 2, 2), v // 2
        near, far = v + 1 - 2 * lax.rem(v, 2), 3 - v
        other = 1 - core
        return (
            (other * near + core * far, other * gray + core * high),
            (other * far + core * near, other * high + core * gray),
        )

    xs = [(y * 4 + v, bit) for v, bit in pairs(x)]
    ys = [(v * 4 + x, bit) for v, bit in pairs(y)]
    return (xs + ys, ys + xs)


def enter(devices):
    barrier = pltpu.get_barrier_semaphore()
    for device in devices:
        pl.semaphore_signal(barrier, inc=1, device_id=device, device_id_type=pl.DeviceIdType.MESH)
    pl.semaphore_wait(barrier, len(devices))


def gram_kernel(p_ref, out_ref, part, half, got, sums, zgot, zsums, whole, core_send, core_recv, dp_send, dp_recv, z_send, z_recv, ag_send, ag_recv, zag_send, zag_recv):
    dp, tensor = lax.axis_index("dp"), lax.axis_index("tensor")
    core, z = lax.rem(tensor, 2), tensor // 2
    nz = lax.axis_size("tensor") // 2
    other = (dp, tensor + 1 - 2 * core)
    steps = dp_steps(core)
    zdev = [(dp, lax.rem(z + d, nz) * 2 + core) for d in range(nz)]
    enter([(partner, tensor) for partner, _ in steps[0]] + zdev[1:] + [other])

    n = p_ref.shape[1]
    nblk = n // NB
    at = 0
    for i in range(nblk):
        prod = mm_tn(p_ref[:, i * NB : (i + 1) * NB], p_ref[:, i * NB :], HI)
        for j in range(nblk - i):
            part[at : at + NB, :] = prod[:, j * NB : (j + 1) * NB]
            at += NB

    rows = at // 2
    mine = pl.multiple_of(core * rows, 8)
    theirs = pl.multiple_of((1 - core) * rows, 8)
    swap = rcopy(part.at[pl.ds(theirs, rows)], half, core_send.at[0], core_recv.at[0], other)
    swap.start()
    swap.wait_recv()
    half[...] = half[...] + part[pl.ds(mine, rows), :]

    length = rows // 2
    offs = [jnp.int32(0), jnp.int32(length)]
    trail = []
    pending = [swap]
    size = length
    got_at = 0
    for k in range(4):
        size //= 2
        copies = []
        for s in range(2):
            partner, bit = steps[s][k]
            keep = pl.multiple_of(offs[s] + bit * size, 8)
            give = pl.multiple_of(offs[s] + (1 - bit) * size, 8)
            copy = rcopy(half.at[pl.ds(give, size)], got.at[s, pl.ds(got_at, size)], dp_send.at[s, k], dp_recv.at[s, k], (partner, tensor))
            copy.start()
            copies.append(copy)
            offs[s] = keep
        for s in range(2):
            copies[s].wait_recv()
            half[pl.ds(offs[s], size), :] = half[pl.ds(offs[s], size), :] + got[s, pl.ds(got_at, size), :]
        trail.append((size, list(offs)))
        pending += copies
        got_at += size

    sums[0:size, :] = half[pl.ds(offs[0], size), :]
    sums[size : 2 * size, :] = half[pl.ds(offs[1], size), :]
    piece = sums.shape[0] // nz
    if sums.shape[0] > 2 * size:
        sums[2 * size :, :] = jnp.zeros((sums.shape[0] - 2 * size, NB), F32)
    copies = []
    for d in range(1, nz):
        zto = lax.rem(z + d, nz)
        copy = rcopy(sums.at[pl.ds(pl.multiple_of(zto * piece, 8), piece)], zgot.at[d], z_send.at[d], z_recv.at[d], zdev[d])
        copy.start()
        copies.append(copy)
    own = pl.multiple_of(z * piece, 8)
    total = sums[pl.ds(own, piece), :]
    for d in range(1, nz):
        copies[d - 1].wait_recv()
        total = total + zgot[d]
    pending += copies
    zsums[pl.ds(own, piece), :] = total
    copies = []
    for d in range(1, nz):
        copy = rcopy(zsums.at[pl.ds(own, piece)], zsums.at[pl.ds(own, piece)], zag_send.at[d], zag_recv.at[d], zdev[d])
        copy.start()
        copies.append(copy)
    for copy in copies:
        copy.wait_recv()
    pending += copies

    for s in range(2):
        whole[pl.ds(pl.multiple_of(mine + offs[s], 8), size), :] = zsums[s * size : (s + 1) * size, :]
    for k in reversed(range(4)):
        size, offs = trail[k]
        copies = []
        for s in range(2):
            region = whole.at[pl.ds(pl.multiple_of(mine + offs[s], 8), size)]
            copy = rcopy(region, region, ag_send.at[s, k], ag_recv.at[s, k], (steps[s][k][0], tensor))
            copy.start()
            copies.append(copy)
        for copy in copies:
            copy.wait_recv()
        pending += copies
    swap = rcopy(whole.at[pl.ds(mine, rows)], whole.at[pl.ds(mine, rows)], core_send.at[1], core_recv.at[1], other)
    swap.start()
    swap.wait_recv()
    pending.append(swap)
    at = 0
    for i in range(nblk):
        for j in range(nblk):
            if j < i:
                out_ref[i * NB : (i + 1) * NB, j * NB : (j + 1) * NB] = jnp.zeros((NB, NB), F32)
            else:
                out_ref[i * NB : (i + 1) * NB, j * NB : (j + 1) * NB] = whole[at : at + NB, :]
                at += NB
    for copy in pending:
        copy.wait_send()


def gram_sum(projected):
    n = projected.shape[1]
    nblk = n // NB
    packed = nblk * (nblk + 1) // 2 * NB
    nz = lax.axis_size("tensor") // 2
    rows = packed // 2
    last = rows // 2 // 16
    piece = -(-2 * last // (8 * nz)) * 8
    dma = pltpu.SemaphoreType.DMA
    return pl.pallas_call(
        gram_kernel,
        out_shape=jax.ShapeDtypeStruct((n, n), F32),
        in_specs=[pl.BlockSpec(memory_space=pltpu.VMEM)],
        out_specs=pl.BlockSpec(memory_space=pltpu.VMEM),
        scratch_shapes=[
            pltpu.VMEM((packed, NB), F32),
            pltpu.VMEM((rows, NB), F32),
            pltpu.VMEM((2, rows // 2, NB), F32),
            pltpu.VMEM((piece * nz, NB), F32),
            pltpu.VMEM((nz, piece, NB), F32),
            pltpu.VMEM((piece * nz, NB), F32),
            pltpu.VMEM((packed, NB), F32),
            dma((2,)), dma((2,)), dma((2, 4)), dma((2, 4)), dma((nz,)), dma((nz,)),
            dma((2, 4)), dma((2, 4)), dma((nz,)), dma((nz,)),
        ],
        compiler_params=pltpu.CompilerParams(
            vmem_limit_bytes=40 << 20, collective_id=1, has_side_effects=True
        ),
        cost_estimate=pl.CostEstimate(flops=30_000_000_000, bytes_accessed=8 << 20, transcendentals=0),
        name="gram_sum",
    )(projected)


def body(buffer, old_basis):
    full_basis = lax.all_gather(old_basis, "dp", axis=1, tiled=True)
    groups = lax.axis_size("tensor")
    rank = full_basis.shape[1]
    share = old_basis.shape[1]
    projected = lax.psum_scatter(
        mm_nn(buffer, full_basis), "tensor", scatter_dimension=0, tiled=True
    )
    gram = gram_sum(projected)

    proj_all = lax.all_gather(projected, "tensor", axis=0, tiled=True)
    proj_hi = lax.reduce_precision(proj_all, 8, 7)
    proj_lo = (proj_all - proj_hi).astype(BF16)
    mixed = mm_tn(buffer, proj_hi.astype(BF16)) + mm_tn(buffer, proj_lo)
    mixed = lax.psum_scatter(mixed, "dp", scatter_dimension=0, tiled=True)

    inverse = chol_inv(gram)
    trans = mm_nt(mixed, inverse, HI)
    squares = lax.psum(jnp.sum(trans * trans, axis=0), ("dp", "tensor"))
    trans_all = lax.all_gather(trans.astype(BF16), "dp", axis=0, tiled=True)
    ortho_all = mm_nt(proj_all, inverse, lax.Precision.HIGH).astype(BF16)
    basis_all = (trans_all.astype(F32) * lax.rsqrt(squares + NORM_EPS)).astype(BF16)
    new_basis = lax.dynamic_slice_in_dim(basis_all, lax.axis_index("dp") * share, share, axis=1)
    feedback = mm_nt(ortho_all, trans_all)
    new_buffer = (buffer.astype(F32) - FEEDBACK_SHARE * feedback).astype(BF16)
    scale_up = math.sqrt(
        buffer.shape[0] * lax.axis_size("dp") * buffer.shape[1] * groups / rank
    )
    product = mm_nt(ortho_all, basis_all)
    weight_update = (-scale_up * product).astype(BF16)
    return (new_buffer, weight_update, new_basis)


def solution(mesh):
    in_specs = (P("dp", "tensor"), P("tensor", "dp"))
    out_specs = (P("dp", "tensor"), P("dp", "tensor"), P("tensor", "dp"))
    return jax.shard_map(body, mesh=mesh, in_specs=in_specs, out_specs=out_specs, check_vma=False)
```

time: 1030 us -> 454 us (0.44)
  waiting for transfers between devices: 603 us -> 173 us
  other arithmetic: 263 us -> 2.16 us
  Pallas kernels: 0 us -> 126 us
  blocking collectives: 25.7 us -> 73.5 us
  local copies, waits for them, and re-layouts: 34.1 us -> 9.29 us
  matrix products: 75.4 us -> 56.1 us
    psum x1 -> x0, waiting for transfers between devices: 269 us -> none  [body(): gram_whole = lax.psum(gram_part, ('dp', 'tensor'))]
    another operation x33 -> x0, other arithmetic: 256 us -> none  [the longest x30 173 us: body(): factor_low = jnp.linalg.cholesky(gram_whole)]
    pallas_call x0 -> x2, Pallas kernels: none -> 126 us  [the longest x1 67.8 us: gram_sum(): pl.pallas_call(gram_kernel, out_shape=jax.ShapeDtypeStruct((n, n), F32),...]
    all_gather x3 -> x2, waiting for transfers between devices: 134 us -> 52.2 us  [the longest x1 52.2 us: body(): proj_all = lax.all_gather(projected, 'tensor', axis=0, tiled=True)]
    reduce_scatter x2 -> x1, waiting for transfers between devices: 144 us -> 65 us  [body(): lax.psum_scatter(mm_nn(buffer, full_basis), 'tensor', scatter_dimension=0...]
    psum x1, blocking collectives: 25.7 us -> 73.5 us  [body(): squares = lax.psum(jnp.sum(trans * trans, axis=0), ('dp', 'tensor'))]
    another operation x29 -> x0, matrix products: 34.5 us -> none  [the longest x14 23.1 us: body(): factor_low = jnp.linalg.cholesky(gram_whole)]
    another operation x34 -> x0, local copies, waits for them, and re-layouts: 25.6 us -> none
  transfers between devices with their start and end apart: 7 -> 5, of which waited for: 7 -> 3; matrix products, arithmetic and copies ran while one was open for 1% -> 3% of each run, Pallas kernels for 0% -> 28%
where the time goes in v1:
time: 454 us
  waiting for transfers between devices  173 us (38%)
  Pallas kernels  126 us (28%)
  blocking collectives  73.5 us (16%)
  matrix products  56.1 us (12%)
  between operations  13.8 us (3%)
  local copies, waits for them, and re-layouts  9.29 us (2%)
    psum x1, blocking collectives, body(): squares = lax.psum(jnp.sum(trans * trans, axis=0), ('dp', 'tensor'))  73.5 us
    pallas_call x1, Pallas kernels, gram_sum(): pl.pallas_call(gram_kernel, out_shape=jax.ShapeDtypeStruct((n, n), F32),...  67.8 us
    reduce_scatter x1, waiting for transfers between devices, body(): lax.psum_scatter(mm_nn(buffer, full_basis), 'tensor', scatter_dimension=0...  65 us
    pallas_call x1, Pallas kernels, chol_inv(): pl.pallas_call(chol_inv_kernel, out_shape=jax.ShapeDtypeStruct((n, n), F3...  57.8 us
    all_gather x1, waiting for transfers between devices, body(): full_basis = lax.all_gather(old_basis, 'dp', axis=1, tiled=True)  55.4 us
    all_gather x1, waiting for transfers between devices, body(): proj_all = lax.all_gather(projected, 'tensor', axis=0, tiled=True)  52.2 us
    dot_general x4, matrix products, mm_nt(): lax.dot_general(a, b, (((1,), (1,)), ((), ())), precision=precision, pref...  35 us
    dot_general x2, matrix products, mm_tn(): lax.dot_general(a, b, (((0,), (0,)), ((), ())), precision=precision, pref...  11.9 us
  transfers between devices with their start and end apart: 5, of which 3 were waited for; matrix products, arithmetic and copies ran while one was open for 3% of the time, Pallas kernels for 28%

profile of v1, /device:TPU:1, one launch (start us, length us, event | category | flops | bytes accessed | tf_op | source)
XLA Modules:
  0.0 454.2 jit_solution(16650066244899664672)
XLA Ops:
  7.2 0.0 all-gather.4.cloned.1.call-start
  7.2 0.7 all-gather.4.cloned.1.call-update
  7.9 0.0 reduce-scatter.5.cloned.1.call-start
  7.9 55.4 %all-gather.4.cloned.1.call-done = bf16[1024,1024]{0,1:T(8,128)(2,1)} async-done(((bf16[1024,64]{0,1:T(8,128)(2,1)}), bf16[1024,1024]{0,1:T(8,128)(2,1)}) %all-gather.4.cloned.1.call-update) | async-done | bytes 2097168 | tf_op jit(solution)/shard_map/all_gather | solution.py:283
  63.4 9.2 %fusion.4 = f32[1664,1024]{1,0:T(8,128)} fusion(bf16[1664,1024]{1,0:T(8,128)(2,1)} %param.2, bf16[1024,1024]{0,1:T(8,128)(2,1)} %all-gather.4.cloned.1.call-done), kind=kOutput, calls=%fused_computation.13 | convolution fusion | flops 3489660928 | bytes 12320768 | tf_op jit(solution)/shard_map/dot_general | solution.py:26
  72.6 0.0 copy-start.3
  72.6 0.0 reduce-scatter.5.cloned.1.call-update
  72.6 0.0 all-gather.6.cloned.1.call-start
  72.6 65.0 %reduce-scatter.5.cloned.1.call-done.p_ref = f32[104,1024]{1,0:T(8,128)} async-done(((f32[1664,1024]{1,0:T(8,128)}), f32[104,1024]{1,0:T(8,128)}) %reduce-scatter.5.cloned.1.call-update) | async-done | bytes 426000 | tf_op jit(solution)/shard_map/reduce_scatter | solution.py:287
  137.6 0.0 all-gather.6.cloned.1.call-update
  137.6 0.0 reduce-scatter.7.cloned.1.call-start
  137.7 52.2 %all-gather.6.cloned.1.call-done = f32[1664,1024]{1,0:T(8,128)} async-done(((f32[104,1024]{1,0:T(8,128)}), f32[1664,1024]{1,0:T(8,128)}) %all-gather.6.cloned.1.call-update) | async-done | bytes 6815760 | tf_op jit(solution)/shard_map/all_gather | solution.py:292
  189.9 0.0 copy-done.3
  189.9 0.0 copy-start.2
  189.9 6.3 %fusion.1 = f32[1024,1024]{1,0:T(8,128)S(1)} fusion(bf16[1664,1024]{1,0:T(8,128)(2,1)S(1)} %copy-done.3, f32[1664,1024]{1,0:T(8,128)} %all-gather.6.cloned.1.call-done), kind=kOutput, calls=%fused_computation.8 | convolution fusion | flops 3494772736 | bytes 14417920 | tf_op jit(solution)/shard_map/dot_general | solution.py:20
  196.2 0.0 copy-done.2
  196.2 5.6 %add_bitcast_fusion = f32[1024,1024]{0,1:T(8,128)} fusion(f32[1024,1024]{1,0:T(8,128)S(1)} %fusion.1, bf16[1664,1024]{1,0:T(8,128)(2,1)S(1)} %copy-done.3, f32[1664,1024]{1,0:T(8,128)S(1)} %copy-done.2), kind=kOutput, calls=%fused_computation.6 | convolution fusion | flops 3494117376 | bytes 18612224 | tf_op jit(solution)/shard_map/dot_general | solution.py:20
  201.8 5.3 %copy.7 = f32[1024,1024]{1,0:T(8,128)} copy(f32[1024,1024]{0,1:T(8,128)} %add_bitcast_fusion) | data formatting | bytes 8388608
  207.2 0.0 copy-start.1
  207.2 0.0 reduce-scatter.7.cloned.1.call-update
  207.2 0.0 all-gather.8.cloned.1.call-start
  207.2 0.9 copy-done.1
  208.2 67.8 %gram_sum.1.g_ref = f32[1024,1024]{1,0:T(8,128)S(1)} custom-call(f32[104,1024]{1,0:T(8,128)S(1)} %copy-done.1), custom_call_target="tpu_custom_call" | custom-call | flops 30000001024 | bytes 8388608 | tf_op jit(solution)/shard_map/gram_sum/pallas_call | solution.py:258
  276.0 57.8 %chol_inv.1 = f32[1024,1024]{1,0:T(8,128)S(1)} custom-call(f32[1024,1024]{1,0:T(8,128)S(1)} %gram_sum.1.g_ref), custom_call_target="tpu_custom_call" | custom-call | flops 60000002048 | bytes 8388608 | tf_op jit(solution)/shard_map/chol_inv/pallas_call | solution.py:99
  333.8 0.0 copy-start
  333.8 2.1 copy-done
  335.9 0.0 reduce-scatter.7.cloned.1.call-done
  335.9 7.0 %multiply_reduce_fusion = (f32[1024]{0:T(1024)S(1)}, bf16[64,1024]{1,0:T(8,128)(2,1)}) fusion(f32[64,1024]{1,0:T(8,128)} %reduce-scatter.7.cloned.1.call-done, f32[1024,1024]{1,0:T(8,128)} %copy-done), kind=kOutput, calls=%fused_computation.10 | convolution fusion | flops 805501952 | bytes 4591616 | tf_op jit(solution)/shard_map/dot_general | solution.py:32
  342.9 0.0 all-gather.8.cloned.1.call-update
  342.9 15.3 %convolution_convert_fusion = bf16[1664,1024]{1,0:T(8,128)(2,1)} fusion(f32[1664,1024]{1,0:T(8,128)} %all-gather.6.cloned.1.call-done, f32[1024,1024]{1,0:T(8,128)} %copy-done), kind=kOutput, calls=%fused_computation.7 | convolution fusion | flops 10470686720 | bytes 14417920 | tf_op jit(solution)/shard_map/dot_general | solution.py:32
  358.2 73.5 %psum.7 = f32[1024]{0:T(1024)S(1)} all-reduce(f32[1024]{0:T(1024)S(1)} %get-tuple-element.9), channel_id=1, replica_groups=mesh['dp'=16,'tensor'=16] {'dp','tensor'}, use_global_device_ids=true, to_apply=%region_3.0 | all-reduce | flops 1024 | bytes 8192 | tf_op jit(solution)/shard_map/psum | solution.py:300
  431.8 0.0 all-gather.8.cloned.1.call-done
  431.8 2.2 multiply_convert_fusion.1
  433.9 0.1 constant_dynamic-slice_fusion
  434.1 0.8 copy.6
  434.9 0.0 copy-start.4
  434.9 0.0 copy-start.5
  434.9 0.0 copy-start.6
  434.9 7.3 %multiply_convert_fusion = bf16[1664,1024]{1,0:T(8,128)(2,1)} fusion(bf16[1664,1024]{1,0:T(8,128)(2,1)} %convolution_convert_fusion, bf16[1024,1024]{1,0:T(8,128)(2,1)S(1)} %multiply_convert_fusion.1), kind=kOutput, calls=%fused_computation.3 | convolution fusion | flops 3493068800 | bytes 8912896 | tf_op jit(solution)/shard_map/dot_general | solution.py:32
  442.2 0.0 copy-done.4
  442.2 0.0 copy-done.5
  442.2 0.0 copy-done.6
  442.2 5.5 %subtract_convert_fusion = bf16[1664,1024]{1,0:T(8,128)(2,1)} fusion(bf16[1664,1024]{1,0:T(8,128)(2,1)S(1)} %copy-done.4, bf16[1664,1024]{1,0:T(8,128)(2,1)S(1)} %copy-done.6, bf16[1024,1024]{1,0:T(8,128)(2,1)S(1)} %copy-done.5), kind=kOutput, calls=%fused_computation.4 | convolution fusion | flops 3496476672 | bytes 12320768 | tf_op jit(solution)/shard_map/dot_general | solution.py:32
  (1 shorter events, 0.0 us)
Async XLA Ops:
  7.2 56.2 %all-gather.4.cloned.1.call-start = ((), (), s32[]{:S(2)}) async-start(), calls=%async_computation.2 | async-start | bytes 2228224 | tf_op jit(solution)/shard_map/all_gather | solution.py:283
  7.9 129.7 %reduce-scatter.5.cloned.1.call-start = ((), (), s32[]{:S(2)}) async-start(), calls=%async_computation.3 | async-start | bytes 7241728 | tf_op jit(solution)/shard_map/reduce_scatter | solution.py:287
  72.6 117.3 %copy-start.3 = (bf16[1664,1024]{1,0:T(8,128)(2,1)S(1)}, bf16[1664,1024]{1,0:T(8,128)(2,1)}, u32[]{:S(2)}) copy-start(bf16[1664,1024]{1,0:T(8,128)(2,1)} %param.2) | copy-start | bytes 10223620
  72.6 117.3 %all-gather.6.cloned.1.call-start = ((), (), s32[]{:S(2)}) async-start(), calls=%async_computation.4 | async-start | bytes 7241728 | tf_op jit(solution)/shard_map/all_gather | solution.py:292
  137.6 198.3 %reduce-scatter.7.cloned.1.call-start = ((), (), s32[]{:S(2)}) async-start(), calls=%async_computation.6 | async-start | bytes 4456448
  189.9 6.3 %copy-start.2 = (f32[1664,1024]{1,0:T(8,128)S(1)}, f32[1664,1024]{1,0:T(8,128)}, u32[]{:S(2)}) copy-start(f32[1664,1024]{1,0:T(8,128)} %all-gather.6.cloned.1.call-done) | copy-start | bytes 20447236
  207.2 1.0 copy-start.1
  207.2 224.6 %all-gather.8.cloned.1.call-start = ((), (), s32[]{:S(2)}) async-start(), calls=%async_computation.5 | async-start | bytes 2228224 | tf_op jit(solution)/shard_map/all_gather | solution.py:301
  333.8 2.1 copy-start
  434.9 7.3 %copy-start.4 = (bf16[1664,1024]{1,0:T(8,128)(2,1)S(1)}, bf16[1664,1024]{1,0:T(8,128)(2,1)}, u32[]{:S(2)}) copy-start(bf16[1664,1024]{1,0:T(8,128)(2,1)} %param.2) | copy-start | bytes 10223620
  434.9 7.3 %copy-start.5 = (bf16[1024,1024]{1,0:T(8,128)(2,1)S(1)}, bf16[1024,1024]{1,0:T(8,128)(2,1)}, u32[]{:S(2)}) copy-start(bf16[1024,1024]{1,0:T(8,128)(2,1)} %all-gather.8.cloned.1.call-done) | copy-start | bytes 6291460
  434.9 7.3 %copy-start.6 = (bf16[1664,1024]{1,0:T(8,128)(2,1)S(1)}, bf16[1664,1024]{1,0:T(8,128)(2,1)}, u32[]{:S(2)}) copy-start(bf16[1664,1024]{1,0:T(8,128)(2,1)} %convolution_convert_fusion) | copy-start | bytes 10223620
Sparse Core Ops, SparseCore 0:
  10.4 52.8 all-gather.3
  72.7 64.8 reduce-scatter.4
  139.5 50.3 all-gather.5
  207.3 80.4 reduce-scatter.6
  343.1 43.8 all-gather.7

commit v2 on v1

--- a/solution.py
+++ b/solution.py
@@ -279,14 +279,278 @@
     )(projected)
 
 
+def dp_offsets(dp, core, length):
+    def bits(v):
+        gray, high = lax.rem(v + v // 2, 2), v // 2
+        other = 1 - core
+        return [other * gray + core * high, other * high + core * gray]
+
+    xs, ys = bits(lax.rem(dp, 4)), bits(dp // 4)
+    out = []
+    for order in (xs + ys, ys + xs):
+        at, size = 0, length
+        for bit in order:
+            size //= 2
+            at = at + bit * size
+        out.append(at)
+    return out
+
+
+def finish_kernel(mixed_ref, inv_ref, proj_ref, ortho_ref, trans_ref, basis_ref, inv_hi, inv_lo, stacked, whole, sq, sq_t, sq_d, sq_sum, ag_send, ag_recv, t_send, t_recv, d_send, d_recv):
+    dp, tensor = lax.axis_index("dp"), lax.axis_index("tensor")
+    ndp, ntensor = lax.axis_size("dp"), lax.axis_size("tensor")
+    core = lax.rem(tensor, 2)
+    steps = dp_steps(core)
+    tdev = [(dp, lax.rem(tensor + d, ntensor)) for d in range(ntensor)]
+    ddev = [(lax.rem(dp + d, ndp), tensor) for d in range(ndp)]
+    enter(tdev[1:] + ddev[1:])
+
+    n = inv_ref.shape[0]
+    for k in range(0, n, 256):
+        wide = inv_ref[k : k + 256, :]
+        high = wide.astype(BF16)
+        inv_hi[k : k + 256, :] = high
+        inv_lo[k : k + 256, :] = (wide - high.astype(F32)).astype(BF16)
+    share = mixed_ref.shape[0]
+    high = mixed_ref[...].astype(BF16)
+    stacked[0:share, :] = high
+    stacked[share:, :] = (mixed_ref[...] - high.astype(F32)).astype(BF16)
+    length = whole.shape[0] // 2
+    offs = dp_offsets(dp, core, length)
+    spots = [pl.multiple_of(s * length + offs[s], 16) for s in range(2)]
+    for k in range(0, n, 256):
+        both = mm_nt(stacked[...], inv_hi[k : k + 256, :])
+        part = both[0:share, :] + both[share:, :] + mm_nt(stacked[0:share, :], inv_lo[k : k + 256, :])
+        squares = jnp.sum(part * part, axis=0, keepdims=True)
+        for j in range(0, 256, NB):
+            sq[(k + j) // NB : (k + j) // NB + 1, :] = squares[:, j : j + NB]
+        part = part.astype(BF16)
+        for s in range(2):
+            whole[pl.ds(spots[s], share // 2), k : k + 256] = part[s * share // 2 : (s + 1) * share // 2, :]
+
+    pending = []
+
+    def gather_step(k):
+        size = length >> (k + 1)
+        copies = []
+        for s in range(2):
+            start = s * length + offs[s] // size * size
+            region = whole.at[pl.ds(pl.multiple_of(start, 16), size)]
+            copy = rcopy(region, region, ag_send.at[s, k], ag_recv.at[s, k], (steps[s][k][0], tensor))
+            copy.start()
+            copies.append(copy)
+        pending.extend(copies)
+        return copies
+
+    def spread(source, slots, send, recv, devices):
+        copies = []
+        for d in range(1, len(devices)):
+            copy = rcopy(source, slots.at[d], send.at[d], recv.at[d], devices[d])
+            copy.start()
+            copies.append(copy)
+        pending.extend(copies)
+        return copies
+
+    def total(source, slots, copies):
+        out = source[...]
+        for d in range(1, slots.shape[0]):
+            copies[d - 1].wait_recv()
+            out = out + slots[d]
+        return out
+
+    def ortho_part(i):
+        rows = proj_ref.shape[0] // 4
+        rows0 = i * rows
+        wide = proj_ref[rows0 : rows0 + rows, :]
+        high = wide.astype(BF16)
+        low = (wide - high.astype(F32)).astype(BF16)
+        for k in range(0, n, 256):
+            e = k + 256
+            hi, lo = inv_hi[k:e, 0:e], inv_lo[k:e, 0:e]
+            value = mm_nt(high[:, 0:e], hi) + (mm_nt(low[:, 0:e], hi) + mm_nt(high[:, 0:e], lo))
+            ortho_ref[rows0 : rows0 + rows, k:e] = value.astype(BF16)
+
+    across = spread(sq, sq_t, t_send, t_recv, tdev)
+    copies = gather_step(3)
+    ortho_part(0)
+    sq_sum[...] = total(sq, sq_t, across)
+    down = spread(sq_sum, sq_d, d_send, d_recv, ddev)
+    for i, k in enumerate((2, 1, 0)):
+        for copy in copies:
+            copy.wait_recv()
+        copies = gather_step(k)
+        ortho_part(i + 1)
+    scale = lax.rsqrt(total(sq_sum, sq_d, down) + NORM_EPS)
+    for copy in copies:
+        copy.wait_recv()
+    half = share // 2
+    for d in range(ndp):
+        there = dp_offsets(jnp.int32(d), core, length)
+        for s in range(2):
+            rows0 = d * share + s * half
+            block = whole[pl.ds(pl.multiple_of(s * length + there[s], 16), half), :]
+            trans_ref[rows0 : rows0 + half, :] = block
+            for j in range(n // NB):
+                basis_ref[rows0 : rows0 + half, j * NB : (j + 1) * NB] = (
+                    block[:, j * NB : (j + 1) * NB].astype(F32) * scale[j : j + 1, :]
+                ).astype(BF16)
+    for copy in pending:
+        copy.wait_send()
+
+
+def finish(mixed, inverse, proj_all):
+    share, n = mixed.shape
+    rows = proj_all.shape[0]
+    ndp, ntensor = lax.axis_size("dp"), lax.axis_size("tensor")
+    dma = pltpu.SemaphoreType.DMA
+    vmem = pl.BlockSpec(memory_space=pltpu.VMEM)
+    return pl.pallas_call(
+        finish_kernel,
+        out_shape=[
+            jax.ShapeDtypeStruct((rows, n), BF16),
+            jax.ShapeDtypeStruct((share * ndp, n), BF16),
+            jax.ShapeDtypeStruct((share * ndp, n), BF16),
+        ],
+        in_specs=[vmem] * 3,
+        out_specs=[vmem] * 3,
+        scratch_shapes=[
+            pltpu.VMEM((n, n), BF16), pltpu.VMEM((n, n), BF16),
+            pltpu.VMEM((2 * share, n), BF16), pltpu.VMEM((share * ndp, n), BF16),
+            pltpu.VMEM((n // NB, NB), F32), pltpu.VMEM((ntensor, n // NB, NB), F32),
+            pltpu.VMEM((ndp, n // NB, NB), F32), pltpu.VMEM((n // NB, NB), F32),
+            dma((2, 4)), dma((2, 4)), dma((ntensor,)), dma((ntensor,)), dma((ndp,)), dma((ndp,)),
+        ],
+        compiler_params=pltpu.CompilerParams(
+            vmem_limit_bytes=48 << 20, collective_id=2, has_side_effects=True
+        ),
+        cost_estimate=pl.CostEstimate(flops=20_000_000_000, bytes_accessed=16 << 20, transcendentals=0),
+        name="finish",
+    )(mixed, inverse, proj_all)
+
+
+def project_kernel(buf_ref, share_ref, out_ref, basis, natural, part, swapped, acc, ring, ag_send, ag_recv, sw_send, sw_recv, ring_send, ring_recv):
+    dp, tensor = lax.axis_index("dp"), lax.axis_index("tensor")
+    ndp, nz = lax.axis_size("dp"), lax.axis_size("tensor") // 2
+    core, z = lax.rem(tensor, 2), tensor // 2
+    other = (dp, tensor + 1 - 2 * core)
+    after = (dp, lax.rem(z + 1 - 2 * core + nz, nz) * 2 + core)
+    before = (dp, lax.rem(z - 1 + 2 * core + nz, nz) * 2 + core)
+    steps = dp_steps(core)
+    enter([(partner, tensor) for partner, _ in steps[0]] + [other, after, before])
+    pending = []
+
+    share = share_ref.shape[0]
+    length = basis.shape[0] // 2
+    offs = dp_offsets(dp, core, length)
+    half = share // 2
+    for s in range(2):
+        basis[pl.ds(pl.multiple_of(s * length + offs[s], 16), half), :] = share_ref[s * half : (s + 1) * half, :]
+    for k in reversed(range(4)):
+        size = length >> (k + 1)
+        copies = []
+        for s in range(2):
+            region = basis.at[pl.ds(pl.multiple_of(s * length + offs[s] // size * size, 16), size)]
+            copy = rcopy(region, region, ag_send.at[s, k], ag_recv.at[s, k], (steps[s][k][0], tensor))
+            copy.start()
+            copies.append(copy)
+        for copy in copies:
+            copy.wait_recv()
+        pending += copies
+    for d in range(ndp):
+        there = dp_offsets(jnp.int32(d), core, length)
+        for s in range(2):
+            rows0 = d * share + s * half
+            natural[rows0 : rows0 + half, :] = basis[pl.ds(pl.multiple_of(s * length + there[s], 16), half), :]
+
+    chunk = buf_ref.shape[0] // nz
+    rows = chunk // 2
+    mine = pl.multiple_of(core * rows, 8)
+    theirs = pl.multiple_of((1 - core) * rows, 8)
+
+    def compute(r):
+        rows0 = pl.multiple_of(lax.rem(z + r, nz) * chunk, 16)
+        for k in range(0, natural.shape[0], 512):
+            part[r, :, k : k + 512] = mm_nt(buf_ref[pl.ds(rows0, chunk), :], natural[k : k + 512, :])
+        copy = rcopy(part.at[r, pl.ds(theirs, rows)], swapped.at[r], sw_send.at[r], sw_recv.at[r], other)
+        copy.start()
+        pending.append(copy)
+
+    columns = out_ref.shape[1] // 2
+
+    def term(r, h):
+        return part[r, pl.ds(mine, rows), h * columns : (h + 1) * columns] + swapped[r, :, h * columns : (h + 1) * columns]
+
+    def swap_wait(r):
+        rcopy(part.at[r, pl.ds(theirs, rows)], swapped.at[r], sw_send.at[r], sw_recv.at[r], other).wait_recv()
+
+    last = [None, None]
+
+    def ring_step(s):
+        r = core * (1 + s) + (1 - core) * (nz - 1 - s)
+        swap_wait(r)
+        for h in range(2):
+            value = term(r, h)
+            if s > 0:
+                last[h].wait_recv()
+                value = value + ring[s - 1, h]
+            acc[s, h] = value
+            last[h] = rcopy(acc.at[s, h], ring.at[s, h], ring_send.at[s, h], ring_recv.at[s, h], after)
+            last[h].start()
+            pending.append(last[h])
+
+    order = []
+    for r in range(1, nz // 2):
+        order += [r, nz - r]
+    order += [nz // 2, 0]
+    done = 0
+    for i in range(0, nz, 2):
+        compute(order[i])
+        compute(order[i + 1])
+        if i >= 2:
+            ring_step(done)
+            done += 1
+    for s in range(done, nz - 1):
+        ring_step(s)
+    swap_wait(0)
+    for h in range(2):
+        value = term(0, h)
+        last[h].wait_recv()
+        out_ref[:, h * columns : (h + 1) * columns] = value + ring[nz - 2, h]
+    for copy in pending:
+        copy.wait_send()
+
+
+def project(buffer, share):
+    nz = lax.axis_size("tensor") // 2
+    n = share.shape[0] * lax.axis_size("dp")
+    depth = share.shape[1]
+    rows = buffer.shape[0] // nz // 2
+    dma = pltpu.SemaphoreType.DMA
+    vmem = pl.BlockSpec(memory_space=pltpu.VMEM)
+    return pl.pallas_call(
+        project_kernel,
+        out_shape=jax.ShapeDtypeStruct((rows, n), F32),
+        in_specs=[vmem] * 2,
+        out_specs=vmem,
+        scratch_shapes=[
+            pltpu.VMEM((n, depth), BF16), pltpu.VMEM((n, depth), BF16),
+            pltpu.VMEM((nz, 2 * rows, n), F32), pltpu.VMEM((nz, rows, n), F32),
+            pltpu.VMEM((nz - 1, 2, rows, n // 2), F32), pltpu.VMEM((nz - 1, 2, rows, n // 2), F32),
+            dma((2, 4)), dma((2, 4)), dma((nz,)), dma((nz,)), dma((nz - 1, 2)), dma((nz - 1, 2)),
+        ],
+        compiler_params=pltpu.CompilerParams(
+            vmem_limit_bytes=48 << 20, collective_id=3, has_side_effects=True
+        ),
+        cost_estimate=pl.CostEstimate(flops=20_000_000_000, bytes_accessed=16 << 20, transcendentals=0),
+        name="project",
+    )(buffer, share)
+
+
 def body(buffer, old_basis):
-    full_basis = lax.all_gather(old_basis, "dp", axis=1, tiled=True)
     groups = lax.axis_size("tensor")
-    rank = full_basis.shape[1]
     share = old_basis.shape[1]
-    projected = lax.psum_scatter(
-        mm_nn(buffer, full_basis), "tensor", scatter_dimension=0, tiled=True
-    )
+    rank = share * lax.axis_size("dp")
+    projected = project(buffer, old_basis.T)
     gram = gram_sum(projected)
 
     proj_all = lax.all_gather(projected, "tensor", axis=0, tiled=True)
@@ -296,11 +560,7 @@
     mixed = lax.psum_scatter(mixed, "dp", scatter_dimension=0, tiled=True)
 
     inverse = chol_inv(gram)
-    trans = mm_nt(mixed, inverse, HI)
-    squares = lax.psum(jnp.sum(trans * trans, axis=0), ("dp", "tensor"))
-    trans_all = lax.all_gather(trans.astype(BF16), "dp", axis=0, tiled=True)
-    ortho_all = mm_nt(proj_all, inverse, lax.Precision.HIGH).astype(BF16)
-    basis_all = (trans_all.astype(F32) * lax.rsqrt(squares + NORM_EPS)).astype(BF16)
+    ortho_all, trans_all, basis_all = finish(mixed, inverse, proj_all)
     new_basis = lax.dynamic_slice_in_dim(basis_all, lax.axis_index("dp") * share, share, axis=1)
     feedback = mm_nt(ortho_all, trans_all)
     new_buffer = (buffer.astype(F32) - FEEDBACK_SHARE * feedback).astype(BF16)

time: 454 us -> 326 us (0.72)
  waiting for transfers between devices: 173 us -> 50.4 us
  Pallas kernels: 126 us -> 230 us
  blocking collectives: 73.5 us -> 0 us
  matrix products: 56.1 us -> 24.7 us
    pallas_call x0 -> x2, Pallas kernels: none -> 103 us  [the longest x1 69.5 us: project(): pl.pallas_call(project_kernel, out_shape=jax.ShapeDtypeStruct((rows, n),...]
    psum x1 -> x0, blocking collectives: 73.5 us -> none  [body(): squares = lax.psum(jnp.sum(trans * trans, axis=0), ('dp', 'tensor'))]
    reduce_scatter x1, waiting for transfers between devices: 65 us -> 0.01 us  [body(): mixed = lax.psum_scatter(mixed, 'dp', scatter_dimension=0, tiled=True)]
    all_gather x2 -> x0, waiting for transfers between devices: 55.4 us -> none  [the longest x1 55.4 us: body(): full_basis = lax.all_gather(old_basis, 'dp', axis=1, tiled=True)]
    dot_general x4 -> x2, matrix products: 35 us -> 12.7 us  [mm_nt(): lax.dot_general(a, b, (((1,), (1,)), ((), ())), precision=precision, pref...]
    dot_general x1 -> x0, matrix products: 9.19 us -> none  [mm_nn(): lax.dot_general(a, b, (((1,), (0,)), ((), ())), precision=precision, pref...]
    unnamed x16 -> x15, local copies, waits for them, and re-layouts: 9.14 us -> 6.68 us
  transfers between devices with their start and end apart: 5 -> 2, of which waited for: 3 -> 1; matrix products, arithmetic and copies ran while one was open for 3% -> 0% of each run, Pallas kernels for 28% -> 39%
where the time goes in v2:
time: 326 us
  Pallas kernels  230 us (71%)
  waiting for transfers between devices  50.4 us (15%)
  matrix products  24.7 us (8%)
  between operations  14.1 us (4%)
  local copies, waits for them, and re-layouts  6.82 us (2%)
    pallas_call x1, Pallas kernels, project(): pl.pallas_call(project_kernel, out_shape=jax.ShapeDtypeStruct((rows, n),...  69.5 us
    pallas_call x1, Pallas kernels, gram_sum(): pl.pallas_call(gram_kernel, out_shape=jax.ShapeDtypeStruct((n, n), F32),...  68.4 us
    pallas_call x1, Pallas kernels, chol_inv(): pl.pallas_call(chol_inv_kernel, out_shape=jax.ShapeDtypeStruct((n, n), F3...  57.9 us
    all_gather x1, waiting for transfers between devices, body(): proj_all = lax.all_gather(projected, 'tensor', axis=0, tiled=True)  50.4 us
    pallas_call x1, Pallas kernels, finish(): pl.pallas_call(finish_kernel, out_shape=[jax.ShapeDtypeStruct((rows, n),...  33.8 us
    dot_general x2, matrix products, mm_nt(): lax.dot_general(a, b, (((1,), (1,)), ((), ())), precision=precision, pref...  12.7 us
    dot_general x2, matrix products, mm_tn(): lax.dot_general(a, b, (((0,), (0,)), ((), ())), precision=precision, pref...  12 us
    unnamed x15, local copies, waits for them, and re-layouts  6.68 us
  transfers between devices with their start and end apart: 2, of which 1 were waited for; matrix products, arithmetic and copies ran while one was open for 0% of the time, Pallas kernels for 39%

profile of v2, /device:TPU:1, one launch (start us, length us, event | category | flops | bytes accessed | tf_op | source)
XLA Modules:
  0.0 325.9 jit_solution(5167082900243902167)
XLA Ops:
  7.2 0.0 all-gather.2.cloned.1.call-start
  7.2 0.0 copy-start
  7.2 2.0 copy-done
  9.2 0.0 copy-start.3
  9.2 0.9 copy-done.3
  10.1 0.0 copy-start.1
  10.1 69.5 %project.1.p_ref = f32[104,1024]{1,0:T(8,128)} custom-call(bf16[1664,1024]{1,0:T(8,128)(2,1)S(1)} %copy-done, bf16[64,1024]{1,0:T(8,128)(2,1)S(1)} %bitcast.9), custom_call_target="tpu_custom_call" | custom-call | flops 20000000000 | bytes 16777216 | tf_op jit(solution)/shard_map/project/pallas_call | solution.py:530
  79.6 0.0 all-gather.2.cloned.1.call-update
  79.7 0.2 reduce-scatter.2.cloned.1.call-start
  79.9 50.4 %all-gather.2.cloned.1.call-done.proj_ref = f32[1664,1024]{1,0:T(8,128)} async-done(((f32[104,1024]{1,0:T(8,128)}), f32[1664,1024]{1,0:T(8,128)}) %all-gather.2.cloned.1.call-update) | async-done | bytes 6815760 | tf_op jit(solution)/shard_map/all_gather | solution.py:556
  130.3 0.0 copy-done.1
  130.3 0.0 copy-start.5
  130.3 6.4 %fusion.1 = f32[1024,1024]{0,1:T(8,128)S(1)} fusion(bf16[1664,1024]{1,0:T(8,128)(2,1)S(1)} %copy-done.1, f32[1664,1024]{1,0:T(8,128)} %all-gather.2.cloned.1.call-done.proj_ref), kind=kOutput, calls=%fused_computation.6 | convolution fusion | flops 3494772736 | bytes 14417920 | tf_op jit(solution)/shard_map/dot_general | solution.py:20
  136.7 0.0 copy-done.5
  136.7 5.6 %add_bitcast_fusion = f32[1024,1024]{1,0:T(8,128)} fusion(f32[1024,1024]{0,1:T(8,128)S(1)} %fusion.1, bf16[1664,1024]{1,0:T(8,128)(2,1)S(1)} %copy-done.1, f32[1664,1024]{1,0:T(8,128)S(1)} %copy-done.5), kind=kOutput, calls=%fused_computation.5 | convolution fusion | flops 3494117376 | bytes 18612224 | tf_op jit(solution)/shard_map/dot_general | solution.py:20
  142.3 0.0 reduce-scatter.2.cloned.1.call-update
  142.3 68.4 %gram_sum.1.g_ref = f32[1024,1024]{1,0:T(8,128)S(1)} custom-call(f32[104,1024]{1,0:T(8,128)} %project.1.p_ref), custom_call_target="tpu_custom_call" | custom-call | flops 30000001024 | bytes 8388608 | tf_op jit(solution)/shard_map/gram_sum/pallas_call | solution.py:258
  210.7 57.9 %chol_inv.1.inv_ref = f32[1024,1024]{1,0:T(8,128)S(1)} custom-call(f32[1024,1024]{1,0:T(8,128)S(1)} %gram_sum.1.g_ref), custom_call_target="tpu_custom_call" | custom-call | flops 60000002048 | bytes 8388608 | tf_op jit(solution)/shard_map/chol_inv/pallas_call | solution.py:99
  268.6 0.0 copy-start.4
  268.6 2.1 copy-done.4
  270.6 0.0 reduce-scatter.2.cloned.1.call-done.mixed_ref
  270.6 0.0 copy-start.2
  270.6 0.9 copy-done.2
  271.6 33.8 %finish.1 = (bf16[1664,1024]{1,0:T(8,128)(2,1)}, bf16[1024,1024]{1,0:T(8,128)(2,1)S(1)}, bf16[1024,1024]{1,0:T(8,128)(2,1)S(1)}) custom-call(f32[64,1024]{1,0:T(8,128)S(1)} %copy-done.2, f32[1024,1024]{1,0:T(8,128)} %copy-done.4, f32[1664,1024]{1,0:T(8,128)} %all-gather.2.cloned.1.call-done.proj_ref), custom_call_target="tpu_custom_call" | custom-call | flops 20000000000 | bytes 16777216 | tf_op jit(solution)/shard_map/finish/pallas_call | solution.py:407
  305.4 0.0 copy-start.6
  305.5 7.3 %multiply_convert_fusion = bf16[1664,1024]{1,0:T(8,128)(2,1)} fusion(bf16[1664,1024]{1,0:T(8,128)(2,1)} %get-tuple-element.6, bf16[1024,1024]{1,0:T(8,128)(2,1)S(1)} %get-tuple-element.8), kind=kOutput, calls=%fused_computation.3 | convolution fusion | flops 3493068800 | bytes 8912896 | tf_op jit(solution)/shard_map/dot_general | solution.py:32
  312.7 0.0 copy-done.6
  312.7 5.4 %subtract_convert_fusion = bf16[1664,1024]{1,0:T(8,128)(2,1)} fusion(bf16[1664,1024]{1,0:T(8,128)(2,1)S(1)} %copy-done.1, bf16[1664,1024]{1,0:T(8,128)(2,1)S(1)} %copy-done.6, bf16[1024,1024]{1,0:T(8,128)(2,1)S(1)} %get-tuple-element.7), kind=kOutput, calls=%fused_computation.4 | convolution fusion | flops 3496476672 | bytes 12320768 | tf_op jit(solution)/shard_map/dot_general | solution.py:32
  318.2 0.1 constant_dynamic-slice_fusion
  318.3 0.8 copy.7
Async XLA Ops:
  7.2 123.1 %all-gather.2.cloned.1.call-start = ((), (), s32[]{:S(2)}) async-start(), calls=%async_computation.1 | async-start | bytes 7241728 | tf_op jit(solution)/shard_map/all_gather | solution.py:556
  7.2 2.0 copy-start
  9.2 0.9 copy-start.3
  10.1 120.2 %copy-start.1 = (bf16[1664,1024]{1,0:T(8,128)(2,1)S(1)}, bf16[1664,1024]{1,0:T(8,128)(2,1)}, u32[]{:S(2)}) copy-start(bf16[1664,1024]{1,0:T(8,128)(2,1)} %buf_ref.1) | copy-start | bytes 10223620
  79.7 191.0 %reduce-scatter.2.cloned.1.call-start = ((), (), s32[]{:S(2)}) async-start(), calls=%async_computation.2 | async-start | bytes 4456448 | tf_op jit(solution)/shard_map/reduce_scatter | solution.py:560
  130.3 6.4 %copy-start.5 = (f32[1664,1024]{1,0:T(8,128)S(1)}, f32[1664,1024]{1,0:T(8,128)}, u32[]{:S(2)}) copy-start(f32[1664,1024]{1,0:T(8,128)} %all-gather.2.cloned.1.call-done.proj_ref) | copy-start | bytes 20447236
  268.6 2.1 copy-start.4
  270.6 1.0 copy-start.2
  305.4 7.3 %copy-start.6 = (bf16[1664,1024]{1,0:T(8,128)(2,1)S(1)}, bf16[1664,1024]{1,0:T(8,128)(2,1)}, u32[]{:S(2)}) copy-start(bf16[1664,1024]{1,0:T(8,128)(2,1)} %get-tuple-element.6) | copy-start | bytes 10223620
Sparse Core Ops, SparseCore 0:
  79.8 50.4 all-gather.1
  142.4 80.1 reduce-scatter.1

commit v3 on v2

--- a/solution.py
+++ b/solution.py
@@ -62,14 +62,14 @@
             block[r0 + MP :, :] = old - update
 
 
-def chol_inv_kernel(g_ref, out_ref, block):
-    n = g_ref.shape[0]
+def chol_inv(out_ref, block, between):
+    n = out_ref.shape[0]
     nblk = n // NB
-    out_ref[...] = g_ref[...]
     lane = lax.broadcasted_iota(jnp.int32, (NB, NB), 1)
     row = lax.broadcasted_iota(jnp.int32, (NB, NB), 0)
 
     def step(k, _):
+        between(k)
         k0 = pl.multiple_of(k * NB, NB)
         block[...] = out_ref[pl.ds(k0, NB), pl.ds(k0, NB)]
         eliminate_block(block)
@@ -94,20 +94,6 @@
         out_ref[k0 : k0 + NB, k0 + NB :] = jnp.zeros((NB, n - k0 - NB), F32)
 
 
-def chol_inv(g):
-    n = g.shape[0]
-    return pl.pallas_call(
-        chol_inv_kernel,
-        out_shape=jax.ShapeDtypeStruct((n, n), F32),
-        in_specs=[pl.BlockSpec(memory_space=pltpu.VMEM)],
-        out_specs=pl.BlockSpec(memory_space=pltpu.VMEM),
-        scratch_shapes=[pltpu.VMEM((NB, NB), F32)],
-        compiler_params=pltpu.CompilerParams(vmem_limit_bytes=40 << 20),
-        cost_estimate=pl.CostEstimate(flops=60_000_000_000, bytes_accessed=8 << 20, transcendentals=0),
-        name="chol_inv",
-    )(g)
-
-
 def rcopy(src, dst, send_sem, recv_sem, device):
     return pltpu.make_async_remote_copy(
         src_ref=src, dst_ref=dst, send_sem=send_sem, recv_sem=recv_sem,
@@ -140,7 +126,7 @@
     pl.semaphore_wait(barrier, len(devices))
 
 
-def gram_kernel(p_ref, out_ref, part, half, got, sums, zgot, zsums, whole, core_send, core_recv, dp_send, dp_recv, z_send, z_recv, ag_send, ag_recv, zag_send, zag_recv):
+def factor_kernel(p_ref, buf_ref, inv_ref, mixed_ref, all_ref, part, half, got, sums, zgot, zsums, whole, block, mixed, mixed_got, core_send, core_recv, dp_send, dp_recv, z_send, z_recv, ag_send, ag_recv, zag_send, zag_recv, plus_send, plus_recv, minus_send, minus_recv, pair_send, pair_recv, w_send, w_recv):
     dp, tensor = lax.axis_index("dp"), lax.axis_index("tensor")
     core, z = lax.rem(tensor, 2), tensor // 2
     nz = lax.axis_size("tensor") // 2
@@ -148,8 +134,67 @@
     steps = dp_steps(core)
     zdev = [(dp, lax.rem(z + d, nz) * 2 + core) for d in range(nz)]
     enter([(partner, tensor) for partner, _ in steps[0]] + zdev[1:] + [other])
-
-    n = p_ref.shape[1]
+    pending = []
+
+    prows, n = p_ref.shape
+
+    def region(r, c):
+        at = (lax.rem(z + r, nz) * 2 + c) * prows
+        return all_ref.at[pl.ds(pl.multiple_of(at, 8), prows)]
+
+    def begin(copy):
+        copy.start()
+        pending.append(copy)
+        return copy
+
+    def pass_on(j):
+        plus = region(nz - j if j else 0, core)
+        begin(rcopy(plus, plus, plus_send.at[j], plus_recv.at[j], zdev[1]))
+        if j < nz // 2 - 1:
+            minus = region(j, core)
+            begin(rcopy(minus, minus, minus_send.at[j], minus_recv.at[j], zdev[nz - 1]))
+
+    def across(r):
+        here = region(r, core)
+        begin(rcopy(here, here, pair_send.at[r], pair_recv.at[r], other))
+
+    def poll(j):
+        here = region(nz - j, core)
+        rcopy(here, here, plus_send.at[j - 1], plus_recv.at[j - 1], zdev[1]).wait_recv()
+        if j < nz // 2:
+            here = region(j, core)
+            rcopy(here, here, minus_send.at[j - 1], minus_recv.at[j - 1], zdev[nz - 1]).wait_recv()
+            pass_on(j)
+            across(j)
+        across(nz - j)
+
+    chunk = 2 * prows
+
+    def accumulate(r):
+        here = region(r, core)
+        rcopy(here, here, pair_send.at[r], pair_recv.at[r], other).wait_recv()
+        rows0 = pl.multiple_of(lax.rem(z + r, nz) * chunk, 16)
+        wide = all_ref[pl.ds(rows0, chunk), :]
+        high = wide.astype(BF16)
+        low = (wide - high.astype(F32)).astype(BF16)
+
+        def strip(i, _):
+            i0 = pl.multiple_of(i * 256, 256)
+            left = buf_ref[pl.ds(rows0, chunk), pl.ds(i0, 256)]
+            for k in range(0, n, 256):
+                value = mm_tn(left, high[:, k : k + 256]) + mm_tn(left, low[:, k : k + 256])
+                if r:
+                    value = value + mixed[pl.ds(i0, 256), k : k + 256]
+                mixed[pl.ds(i0, 256), k : k + 256] = value
+            return 0
+
+        lax.fori_loop(0, mixed.shape[0] // 256, strip, 0)
+
+    own_rows = pl.multiple_of(tensor * prows, 8)
+    all_ref[pl.ds(own_rows, prows), :] = p_ref[...]
+    pass_on(0)
+    across(0)
+
     nblk = n // NB
     at = 0
     for i in range(nblk):
@@ -161,15 +206,13 @@
     rows = at // 2
     mine = pl.multiple_of(core * rows, 8)
     theirs = pl.multiple_of((1 - core) * rows, 8)
-    swap = rcopy(part.at[pl.ds(theirs, rows)], half, core_send.at[0], core_recv.at[0], other)
-    swap.start()
+    swap = begin(rcopy(part.at[pl.ds(theirs, rows)], half, core_send.at[0], core_recv.at[0], other))
     swap.wait_recv()
     half[...] = half[...] + part[pl.ds(mine, rows), :]
 
     length = rows // 2
     offs = [jnp.int32(0), jnp.int32(length)]
     trail = []
-    pending = [swap]
     size = length
     got_at = 0
     for k in range(4):
@@ -179,15 +222,18 @@
             partner, bit = steps[s][k]
             keep = pl.multiple_of(offs[s] + bit * size, 8)
             give = pl.multiple_of(offs[s] + (1 - bit) * size, 8)
-            copy = rcopy(half.at[pl.ds(give, size)], got.at[s, pl.ds(got_at, size)], dp_send.at[s, k], dp_recv.at[s, k], (partner, tensor))
-            copy.start()
-            copies.append(copy)
+            copies.append(begin(rcopy(half.at[pl.ds(give, size)], got.at[s, pl.ds(got_at, size)], dp_send.at[s, k], dp_recv.at[s, k], (partner, tensor))))
             offs[s] = keep
+        if k == 0:
+            accumulate(0)
+        elif k >= 2:
+            accumulate((1, nz - 1)[k - 2])
         for s in range(2):
             copies[s].wait_recv()
             half[pl.ds(offs[s], size), :] = half[pl.ds(offs[s], size), :] + got[s, pl.ds(got_at, size), :]
+        if k == 0:
+            poll(1)
         trail.append((size, list(offs)))
-        pending += copies
         got_at += size
 
     sums[0:size, :] = half[pl.ds(offs[0], size), :]
@@ -198,24 +244,19 @@
     copies = []
     for d in range(1, nz):
         zto = lax.rem(z + d, nz)
-        copy = rcopy(sums.at[pl.ds(pl.multiple_of(zto * piece, 8), piece)], zgot.at[d], z_send.at[d], z_recv.at[d], zdev[d])
-        copy.start()
-        copies.append(copy)
+        copies.append(begin(rcopy(sums.at[pl.ds(pl.multiple_of(zto * piece, 8), piece)], zgot.at[d], z_send.at[d], z_recv.at[d], zdev[d])))
+    poll(2)
     own = pl.multiple_of(z * piece, 8)
     total = sums[pl.ds(own, piece), :]
     for d in range(1, nz):
         copies[d - 1].wait_recv()
         total = total + zgot[d]
-    pending += copies
     zsums[pl.ds(own, piece), :] = total
     copies = []
     for d in range(1, nz):
-        copy = rcopy(zsums.at[pl.ds(own, piece)], zsums.at[pl.ds(own, piece)], zag_send.at[d], zag_recv.at[d], zdev[d])
-        copy.start()
-        copies.append(copy)
+        copies.append(begin(rcopy(zsums.at[pl.ds(own, piece)], zsums.at[pl.ds(own, piece)], zag_send.at[d], zag_recv.at[d], zdev[d])))
     for copy in copies:
         copy.wait_recv()
-    pending += copies
 
     for s in range(2):
         whole[pl.ds(pl.multiple_of(mine + offs[s], 8), size), :] = zsums[s * size : (s + 1) * size, :]
@@ -223,43 +264,92 @@
         size, offs = trail[k]
         copies = []
         for s in range(2):
-            region = whole.at[pl.ds(pl.multiple_of(mine + offs[s], 8), size)]
-            copy = rcopy(region, region, ag_send.at[s, k], ag_recv.at[s, k], (steps[s][k][0], tensor))
-            copy.start()
-            copies.append(copy)
+            here = whole.at[pl.ds(pl.multiple_of(mine + offs[s], 8), size)]
+            copies.append(begin(rcopy(here, here, ag_send.at[s, k], ag_recv.at[s, k], (steps[s][k][0], tensor))))
+        if k == 2:
+            poll(3)
+        accumulate((nz - 3, 3, nz - 2, 2)[k])
         for copy in copies:
             copy.wait_recv()
-        pending += copies
-    swap = rcopy(whole.at[pl.ds(mine, rows)], whole.at[pl.ds(mine, rows)], core_send.at[1], core_recv.at[1], other)
-    swap.start()
+    swap = begin(rcopy(whole.at[pl.ds(mine, rows)], whole.at[pl.ds(mine, rows)], core_send.at[1], core_recv.at[1], other))
+    poll(4)
+    accumulate(4)
     swap.wait_recv()
-    pending.append(swap)
+
+    wlen = mixed.shape[0] // 2
+    woffs = dp_offsets(dp, core, wlen)
+
+    def mixed_copy(k, s):
+        size = wlen >> (k + 1)
+        partner, bit = steps[s][k]
+        keep = s * wlen + woffs[s] // size * size
+        give = keep + (1 - 2 * bit) * size
+        slot = mixed_got.at[s, pl.ds(wlen - 2 * size, size)]
+        return rcopy(mixed.at[pl.ds(pl.multiple_of(give, 8), size)], slot, w_send.at[s, k], w_recv.at[s, k], (partner, tensor)), keep, size
+
+    def mixed_add(k):
+        for s in range(2):
+            copy, keep, size = mixed_copy(k, s)
+            copy.wait_recv()
+            rows = pl.ds(pl.multiple_of(keep, 8), size)
+            mixed[rows, :] = mixed[rows, :] + mixed_got[s, wlen - 2 * size : wlen - size, :]
+
+    def mixed_send(k):
+        for s in range(2):
+            mixed_copy(k, s)[0].start()
+
+    mixed_send(0)
+
     at = 0
     for i in range(nblk):
         for j in range(nblk):
             if j < i:
-                out_ref[i * NB : (i + 1) * NB, j * NB : (j + 1) * NB] = jnp.zeros((NB, NB), F32)
+                inv_ref[i * NB : (i + 1) * NB, j * NB : (j + 1) * NB] = jnp.zeros((NB, NB), F32)
             else:
-                out_ref[i * NB : (i + 1) * NB, j * NB : (j + 1) * NB] = whole[at : at + NB, :]
+                inv_ref[i * NB : (i + 1) * NB, j * NB : (j + 1) * NB] = whole[at : at + NB, :]
                 at += NB
+
+    def between(k):
+        for phase in range(3):
+            @pl.when(k == phase + 2)
+            def _():
+                mixed_add(phase)
+                mixed_send(phase + 1)
+
+    chol_inv(inv_ref, block, between)
+
+    mixed_add(3)
+    size = wlen >> 4
+    for s in range(2):
+        mixed_ref[s * size : (s + 1) * size, :] = mixed[pl.ds(pl.multiple_of(s * wlen + woffs[s], 8), size), :]
+    for k in range(4):
+        for s in range(2):
+            mixed_copy(k, s)[0].wait_send()
     for copy in pending:
         copy.wait_send()
 
 
-def gram_sum(projected):
-    n = projected.shape[1]
+def factor(projected, buffer):
+    prows, n = projected.shape
+    depth = buffer.shape[1]
     nblk = n // NB
     packed = nblk * (nblk + 1) // 2 * NB
     nz = lax.axis_size("tensor") // 2
+    ndp = lax.axis_size("dp")
     rows = packed // 2
     last = rows // 2 // 16
     piece = -(-2 * last // (8 * nz)) * 8
     dma = pltpu.SemaphoreType.DMA
+    vmem = pl.BlockSpec(memory_space=pltpu.VMEM)
     return pl.pallas_call(
-        gram_kernel,
-        out_shape=jax.ShapeDtypeStruct((n, n), F32),
-        in_specs=[pl.BlockSpec(memory_space=pltpu.VMEM)],
-        out_specs=pl.BlockSpec(memory_space=pltpu.VMEM),
+        factor_kernel,
+        out_shape=[
+            jax.ShapeDtypeStruct((n, n), F32),
+            jax.ShapeDtypeStruct((depth // ndp, n), F32),
+            jax.ShapeDtypeStruct((prows * 2 * nz, n), F32),
+        ],
+        in_specs=[vmem] * 2,
+        out_specs=[vmem] * 3,
         scratch_shapes=[
             pltpu.VMEM((packed, NB), F32),
             pltpu.VMEM((rows, NB), F32),
@@ -268,15 +358,20 @@
             pltpu.VMEM((nz, piece, NB), F32),
             pltpu.VMEM((piece * nz, NB), F32),
             pltpu.VMEM((packed, NB), F32),
+            pltpu.VMEM((NB, NB), F32),
+            pltpu.VMEM((depth, n), F32),
+            pltpu.VMEM((2, depth // 2, n), F32),
             dma((2,)), dma((2,)), dma((2, 4)), dma((2, 4)), dma((nz,)), dma((nz,)),
             dma((2, 4)), dma((2, 4)), dma((nz,)), dma((nz,)),
+            dma((nz // 2,)), dma((nz // 2,)), dma((nz // 2,)), dma((nz // 2,)), dma((nz,)), dma((nz,)),
+            dma((2, 4)), dma((2, 4)),
         ],
         compiler_params=pltpu.CompilerParams(
-            vmem_limit_bytes=40 << 20, collective_id=1, has_side_effects=True
+            vmem_limit_bytes=56 << 20, collective_id=1, has_side_effects=True
         ),
-        cost_estimate=pl.CostEstimate(flops=30_000_000_000, bytes_accessed=8 << 20, transcendentals=0),
-        name="gram_sum",
-    )(projected)
+        cost_estimate=pl.CostEstimate(flops=60_000_000_000, bytes_accessed=24 << 20, transcendentals=0),
+        name="factor",
+    )(projected, buffer)
 
 
 def dp_offsets(dp, core, length):
@@ -383,17 +478,13 @@
     scale = lax.rsqrt(total(sq_sum, sq_d, down) + NORM_EPS)
     for copy in copies:
         copy.wait_recv()
-    half = share // 2
-    for d in range(ndp):
-        there = dp_offsets(jnp.int32(d), core, length)
-        for s in range(2):
-            rows0 = d * share + s * half
-            block = whole[pl.ds(pl.multiple_of(s * length + there[s], 16), half), :]
-            trans_ref[rows0 : rows0 + half, :] = block
-            for j in range(n // NB):
-                basis_ref[rows0 : rows0 + half, j * NB : (j + 1) * NB] = (
-                    block[:, j * NB : (j + 1) * NB].astype(F32) * scale[j : j + 1, :]
-                ).astype(BF16)
+    for rows0 in range(0, whole.shape[0], NB):
+        block = whole[rows0 : rows0 + NB, :]
+        trans_ref[rows0 : rows0 + NB, :] = block
+        for j in range(n // NB):
+            basis_ref[rows0 : rows0 + NB, j * NB : (j + 1) * NB] = (
+                block[:, j * NB : (j + 1) * NB].astype(F32) * scale[j : j + 1, :]
+            ).astype(BF16)
     for copy in pending:
         copy.wait_send()
 
@@ -551,15 +642,7 @@
     share = old_basis.shape[1]
     rank = share * lax.axis_size("dp")
     projected = project(buffer, old_basis.T)
-    gram = gram_sum(projected)
-
-    proj_all = lax.all_gather(projected, "tensor", axis=0, tiled=True)
-    proj_hi = lax.reduce_precision(proj_all, 8, 7)
-    proj_lo = (proj_all - proj_hi).astype(BF16)
-    mixed = mm_tn(buffer, proj_hi.astype(BF16)) + mm_tn(buffer, proj_lo)
-    mixed = lax.psum_scatter(mixed, "dp", scatter_dimension=0, tiled=True)
-
-    inverse = chol_inv(gram)
+    inverse, mixed, proj_all = factor(projected, buffer)
     ortho_all, trans_all, basis_all = finish(mixed, inverse, proj_all)
     new_basis = lax.dynamic_slice_in_dim(basis_all, lax.axis_index("dp") * share, share, axis=1)
     feedback = mm_nt(ortho_all, trans_all)

time: 326 us -> 258 us (0.79)
  waiting for transfers between devices: 50.4 us -> 0 us
  between operations: 14.1 us -> 0.7 us
  matrix products: 24.7 us -> 12.7 us
  Pallas kernels: 230 us -> 239 us
    all_gather x1 -> x0, waiting for transfers between devices: 50.4 us -> none  [body(): proj_all = lax.all_gather(projected, 'tensor', axis=0, tiled=True)]
    dot_general x2 -> x0, matrix products: 12 us -> none  [mm_tn(): lax.dot_general(a, b, (((0,), (0,)), ((), ())), precision=precision, pref...]
    pallas_call x2 -> x1, Pallas kernels: 126 us -> 136 us  [factor(): pl.pallas_call(factor_kernel, out_shape=[jax.ShapeDtypeStruct((n, n), F32...]
    unnamed x15 -> x13, local copies, waits for them, and re-layouts: 6.68 us -> 5.35 us
  transfers between devices with their start and end apart: 2 -> 0, of which waited for: 1 -> 0; matrix products, arithmetic and copies ran while one was open for 0% -> 0% of each run, Pallas kernels for 39% -> 0%
where the time goes in v3:
time: 258 us
  Pallas kernels  239 us (93%)
  matrix products  12.7 us (5%)
  local copies, waits for them, and re-layouts  5.5 us (2%)
    pallas_call x1, Pallas kernels, factor(): pl.pallas_call(factor_kernel, out_shape=[jax.ShapeDtypeStruct((n, n), F32...  136 us
    pallas_call x1, Pallas kernels, project(): pl.pallas_call(project_kernel, out_shape=jax.ShapeDtypeStruct((rows, n),...  68.8 us
    pallas_call x1, Pallas kernels, finish(): pl.pallas_call(finish_kernel, out_shape=[jax.ShapeDtypeStruct((rows, n),...  34 us
    dot_general x2, matrix products, mm_nt(): lax.dot_general(a, b, (((1,), (1,)), ((), ())), precision=precision, pref...  12.7 us
    unnamed x13, local copies, waits for them, and re-layouts  5.35 us

profile of v3, /device:TPU:1, one launch (start us, length us, event | category | flops | bytes accessed | tf_op | source)
XLA Modules:
  0.0 258.0 jit_solution(3117552624974844233)
XLA Ops:
  0.6 0.0 copy-start
  0.6 2.0 copy-done
  2.6 0.0 copy-start.2
  2.6 0.9 copy-done.2
  3.5 68.8 %project.1.p_ref = f32[104,1024]{1,0:T(8,128)S(1)} custom-call(bf16[1664,1024]{1,0:T(8,128)(2,1)S(1)} %copy-done, bf16[64,1024]{1,0:T(8,128)(2,1)S(1)} %bitcast.5), custom_call_target="tpu_custom_call" | custom-call | flops 20000000000 | bytes 16777216 | tf_op jit(solution)/shard_map/project/pallas_call | solution.py:621
  72.3 0.0 copy-start.3
  72.3 0.7 copy-done.3
  73.0 136.3 %factor.1 = (f32[1024,1024]{1,0:T(8,128)}, f32[64,1024]{1,0:T(8,128)}, f32[1664,1024]{1,0:T(8,128)}) custom-call(f32[104,1024]{1,0:T(8,128)} %copy-done.3, bf16[1664,1024]{1,0:T(8,128)(2,1)} %buf_ref.3), custom_call_target="tpu_custom_call" | custom-call | flops 60000002048 | bytes 25165824 | tf_op jit(solution)/shard_map/factor/pallas_call | solution.py:344
  209.4 0.0 copy-start.4
  209.4 0.9 copy-done.4
  210.3 34.0 %finish.1 = (bf16[1664,1024]{1,0:T(8,128)(2,1)}, bf16[1024,1024]{1,0:T(8,128)(2,1)S(1)}, bf16[1024,1024]{1,0:T(8,128)(2,1)S(1)}) custom-call(f32[64,1024]{1,0:T(8,128)S(1)} %copy-done.4, f32[1024,1024]{1,0:T(8,128)} %get-tuple-element.10.inv_ref, f32[1664,1024]{1,0:T(8,128)} %get-tuple-element.11.proj_ref), custom_call_target="tpu_custom_call" | custom-call | flops 20000000000 | bytes 16777216 | tf_op jit(solution)/shard_map/finish/pallas_call | solution.py:498
  244.3 0.0 copy-start.1
  244.4 0.0 copy-start.5
  244.4 7.3 %multiply_convert_fusion = bf16[1664,1024]{1,0:T(8,128)(2,1)} fusion(bf16[1664,1024]{1,0:T(8,128)(2,1)} %get-tuple-element.12, bf16[1024,1024]{1,0:T(8,128)(2,1)S(1)} %get-tuple-element.14), kind=kOutput, calls=%fused_computation | convolution fusion | flops 3493068800 | bytes 8912896 | tf_op jit(solution)/shard_map/dot_general | solution.py:32
  251.7 0.0 copy-done.1
  251.7 0.0 copy-done.5
  251.7 5.4 %subtract_convert_fusion = bf16[1664,1024]{1,0:T(8,128)(2,1)} fusion(bf16[1664,1024]{1,0:T(8,128)(2,1)S(1)} %copy-done.1, bf16[1664,1024]{1,0:T(8,128)(2,1)S(1)} %copy-done.5, bf16[1024,1024]{1,0:T(8,128)(2,1)S(1)} %get-tuple-element.13), kind=kOutput, calls=%fused_computation.1 | convolution fusion | flops 3496476672 | bytes 12320768 | tf_op jit(solution)/shard_map/dot_general | solution.py:32
  257.0 0.1 constant_dynamic-slice_fusion
  257.2 0.8 copy.5
Async XLA Ops:
  0.6 2.0 copy-start
  2.6 0.9 copy-start.2
  72.3 0.8 copy-start.3
  209.4 1.0 copy-start.4
  244.3 7.3 %copy-start.1 = (bf16[1664,1024]{1,0:T(8,128)(2,1)S(1)}, bf16[1664,1024]{1,0:T(8,128)(2,1)}, u32[]{:S(2)}) copy-start(bf16[1664,1024]{1,0:T(8,128)(2,1)} %buf_ref.3) | copy-start | bytes 10223620
  244.4 7.3 %copy-start.5 = (bf16[1664,1024]{1,0:T(8,128)(2,1)S(1)}, bf16[1664,1024]{1,0:T(8,128)(2,1)}, u32[]{:S(2)}) copy-start(bf16[1664,1024]{1,0:T(8,128)(2,1)} %get-tuple-element.12) | copy-start | bytes 10223620

commit v4 on v3

--- a/solution.py
+++ b/solution.py
@@ -13,7 +13,7 @@
 F32 = jnp.float32
 BF16 = jnp.bfloat16
 NB = 128
-MP = 16
+MP = 32
 
 
 def mm_tn(a, b, precision=None):
@@ -34,20 +34,50 @@
     )
 
 
+def three(x):
+    h = x.astype(BF16)
+    rest = x - h.astype(F32)
+    m = rest.astype(BF16)
+    return h, m, (rest - m.astype(F32)).astype(BF16)
+
+
 def eliminate_rows(rows, r0):
-    lane = lax.broadcasted_iota(jnp.int32, (MP, NB), 1)
-    row = lax.broadcasted_iota(jnp.int32, (MP, NB), 0)
-    cols = [jnp.broadcast_to(rows[:, r0 + c : r0 + c + 1], (MP, NB)) for c in range(MP)]
-    scale = jnp.zeros((MP, NB), F32)
+    lane = lax.broadcasted_iota(jnp.int32, (8, NB), 1)
+    row = lax.broadcasted_iota(jnp.int32, (8, NB), 0)
+    groups = MP // 8
+    parts = [rows[8 * g : 8 * g + 8, :] for g in range(groups)]
+    cols = [
+        [jnp.broadcast_to(parts[g][:, r0 + c : r0 + c + 1], (8, NB)) if g >= c // 8 else None for g in range(groups)]
+        for c in range(MP)
+    ]
+    scales = [jnp.zeros((8, NB), F32) for _ in range(groups)]
+
+    def spread(value, i):
+        return jnp.broadcast_to(value[i : i + 1, :], (8, NB))
+
     for c in range(MP):
-        rs = lax.rsqrt(cols[c][c : c + 1, :])
-        f = jnp.where(row > c, cols[c] * (rs * rs), 0.0)
-        rows = jnp.where(lane == r0 + c, jnp.where(row == c, 1.0, 0.0), rows)
+        own, at = c // 8, c % 8
+        rs = lax.rsqrt(spread(cols[c][own], at))
+        inv = rs * rs
+        f = [None] * groups
+        for g in range(own, groups):
+            f[g] = cols[c][g] * inv
+        f[own] = jnp.where(row > at, f[own], 0.0)
         for c2 in range(c + 1, MP):
-            cols[c2] = cols[c2] - f * cols[c2][c : c + 1, :]
-        rows = rows - f * rows[c : c + 1, :]
-        scale = jnp.where(row == c, rs, scale)
-    return rows * scale
+            e = spread(cols[c][c2 // 8], c2 % 8)
+            for g in range(c2 // 8, groups):
+                cols[c2][g] = cols[c2][g] - f[g] * e
+        pivot = jnp.where(lane == r0 + c, 1.0, spread(parts[own], at))
+        for g in range(groups):
+            if g < own:
+                parts[g] = jnp.where(lane == r0 + c, 0.0, parts[g])
+            else:
+                kept = jnp.where(lane == r0 + c, 0.0, parts[g])
+                if g == own:
+                    kept = jnp.where(row == at, pivot, kept)
+                parts[g] = kept - f[g] * pivot
+        scales[own] = jnp.where(row == at, rs, scales[own])
+    return jnp.concatenate([p * v for p, v in zip(parts, scales)], axis=0)
 
 
 def eliminate_block(block):
@@ -56,13 +86,16 @@
         rows = eliminate_rows(block[r0 : r0 + MP, :], r0)
         block[r0 : r0 + MP, :] = rows
         if r0 + MP < NB:
-            update = mm_tn(rows, rows, HI)[r0 + MP :, :]
+            h, m, l = three(rows)
+            left = jnp.concatenate([h, h, m, h, l, m], axis=0)
+            right = jnp.concatenate([h, m, h, l, h, m], axis=0)
+            update = mm_tn(left, right)[r0 + MP :, :]
             below = lane[r0 + MP :, :]
             old = jnp.where((below >= r0) & (below < r0 + MP), 0.0, block[r0 + MP :, :])
             block[r0 + MP :, :] = old - update
 
 
-def chol_inv(out_ref, block, between):
+def chol_inv(out_ref, block, left, right, between):
     n = out_ref.shape[0]
     nblk = n // NB
     lane = lax.broadcasted_iota(jnp.int32, (NB, NB), 1)
@@ -76,17 +109,26 @@
         linv = jnp.where(lane <= row, block[...], 0.0)
         out_ref[pl.ds(k0, NB), :] = mm_nn(linv, out_ref[pl.ds(k0, NB), :], HI)
         out_ref[pl.ds(k0, NB), pl.ds(k0, NB)] = linv
-
-        def below(i, _):
-            i0 = pl.multiple_of(i * NB, NB)
-            u = out_ref[pl.ds(k0, NB), pl.ds(i0, NB)]
-            out_ref[pl.ds(i0, NB), pl.ds(k0, NB)] = jnp.zeros((NB, NB), F32)
-            out_ref[pl.ds(i0, NB), :] = out_ref[pl.ds(i0, NB), :] - mm_tn(
-                u, out_ref[pl.ds(k0, NB), :], HI
+        h, m, l = three(out_ref[pl.ds(k0, NB), :])
+        for j, (a, b) in enumerate(zip((h, h, m, h, l, m), (h, m, h, l, h, m))):
+            left[j * NB : (j + 1) * NB, :] = a
+            right[j * NB : (j + 1) * NB, :] = b
+
+        def below(i0, size):
+            out_ref[pl.ds(i0, size), pl.ds(k0, NB)] = jnp.zeros((size, NB), F32)
+            out_ref[pl.ds(i0, size), :] = out_ref[pl.ds(i0, size), :] - mm_tn(
+                left[:, pl.ds(i0, size)], right[...]
             )
+
+        @pl.when(lax.rem(k, 2) == 0)
+        def _():
+            below(pl.multiple_of(k0 + NB, NB), NB)
+
+        def pair(i, _):
+            below(pl.multiple_of(i * 2 * NB, 2 * NB), 2 * NB)
             return 0
 
-        lax.fori_loop(k + 1, nblk, below, 0)
+        lax.fori_loop(k // 2 + 1, nblk // 2, pair, 0)
         return 0
 
     lax.fori_loop(0, nblk, step, 0)
@@ -126,14 +168,36 @@
     pl.semaphore_wait(barrier, len(devices))
 
 
-def factor_kernel(p_ref, buf_ref, inv_ref, mixed_ref, all_ref, part, half, got, sums, zgot, zsums, whole, block, mixed, mixed_got, core_send, core_recv, dp_send, dp_recv, z_send, z_recv, ag_send, ag_recv, zag_send, zag_recv, plus_send, plus_recv, minus_send, minus_recv, pair_send, pair_recv, w_send, w_recv):
+def dp_offsets(dp, core, length):
+    def bits(v):
+        gray, high = lax.rem(v + v // 2, 2), v // 2
+        other = 1 - core
+        return [other * gray + core * high, other * high + core * gray]
+
+    xs, ys = bits(lax.rem(dp, 4)), bits(dp // 4)
+    out = []
+    for order in (xs + ys, ys + xs):
+        at, size = 0, length
+        for bit in order:
+            size //= 2
+            at = at + bit * size
+        out.append(at)
+    return out
+
+
+def factor_kernel(
+    p_ref, buf_ref, ortho_ref, trans_ref, basis_ref, inv_ref, all_ref, left, right, inv_hi, inv_lo, stacked, part, half, got, sums, zgot, zsums, whole, block, mixed, mixed_got, sq, sq_t, sq_d, sq_sum, core_send, core_recv, dp_send, dp_recv, z_send, z_recv, ag_send, ag_recv, zag_send, zag_recv, plus_send, plus_recv, minus_send, minus_recv, pair_send, pair_recv, w_send, w_recv, tr_send, tr_recv, t_send, t_recv, d_send, d_recv,
+):
     dp, tensor = lax.axis_index("dp"), lax.axis_index("tensor")
     core, z = lax.rem(tensor, 2), tensor // 2
     nz = lax.axis_size("tensor") // 2
     other = (dp, tensor + 1 - 2 * core)
     steps = dp_steps(core)
+    ndp, ntensor = lax.axis_size("dp"), 2 * nz
     zdev = [(dp, lax.rem(z + d, nz) * 2 + core) for d in range(nz)]
-    enter([(partner, tensor) for partner, _ in steps[0]] + zdev[1:] + [other])
+    tdev = [(dp, lax.rem(tensor + d, ntensor)) for d in range(ntensor)]
+    ddev = [(lax.rem(dp + d, ndp), tensor) for d in range(ndp)]
+    enter(tdev[1:] + ddev[1:])
     pending = []
 
     prows, n = p_ref.shape
@@ -196,17 +260,41 @@
     across(0)
 
     nblk = n // NB
-    at = 0
-    for i in range(nblk):
-        prod = mm_tn(p_ref[:, i * NB : (i + 1) * NB], p_ref[:, i * NB :], HI)
-        for j in range(nblk - i):
-            part[at : at + NB, :] = prod[:, j * NB : (j + 1) * NB]
-            at += NB
-
-    rows = at // 2
+    order = [[0, 1, nblk - 2, nblk - 1], list(range(2, nblk - 2))]
+    spots = {}
+    for i in order[0] + order[1]:
+        for j in range(i, nblk):
+            spots[i, j] = len(spots) * NB
+    rows = len(spots) * NB // 2
     mine = pl.multiple_of(core * rows, 8)
     theirs = pl.multiple_of((1 - core) * rows, 8)
-    swap = begin(rcopy(part.at[pl.ds(theirs, rows)], half, core_send.at[0], core_recv.at[0], other))
+    deep = -(-prows // 16) * 16
+    padded = jnp.concatenate([p_ref[...], jnp.zeros((deep - prows, n), F32)], axis=0)
+    h, m, l = three(padded)
+    for j, (a, b) in enumerate(zip((h, h, m, h, l, m), (h, m, h, l, h, m))):
+        left[j * deep : (j + 1) * deep, :] = a
+        right[j * deep : (j + 1) * deep, :] = b
+
+    def gram_half(which):
+        for i in order[which][::2]:
+            i0 = i * NB
+            prod = mm_tn(left[0 : 6 * deep, i0 : i0 + 2 * NB], right[0 : 6 * deep, i0:])
+            for i2 in (i, i + 1):
+                for j in range(i2, nblk):
+                    at = spots[i2, j]
+                    part[at : at + NB, :] = prod[(i2 - i) * NB : (i2 - i + 1) * NB, (j - i) * NB : (j - i + 1) * NB]
+
+    for c in range(2):
+        @pl.when(core == c)
+        def _():
+            gram_half(1 - c)
+
+    swap = begin(rcopy(part.at[pl.ds(theirs, rows)], half, core_send.at[0, 0], core_recv.at[0, 0], other))
+    for c in range(2):
+        @pl.when(core == c)
+        def _():
+            gram_half(c)
+
     swap.wait_recv()
     half[...] = half[...] + part[pl.ds(mine, rows), :]
 
@@ -258,8 +346,14 @@
     for copy in copies:
         copy.wait_recv()
 
+    def to_other(stage, s, start, count):
+        here = whole.at[pl.ds(pl.multiple_of(mine + start, 8), count)]
+        return begin(rcopy(here, here, core_send.at[s, stage], core_recv.at[s, stage], other))
+
+    passed = []
     for s in range(2):
         whole[pl.ds(pl.multiple_of(mine + offs[s], 8), size), :] = zsums[s * size : (s + 1) * size, :]
+        passed.append(to_other(1, s, offs[s], size))
     for k in reversed(range(4)):
         size, offs = trail[k]
         copies = []
@@ -269,12 +363,13 @@
         if k == 2:
             poll(3)
         accumulate((nz - 3, 3, nz - 2, 2)[k])
-        for copy in copies:
-            copy.wait_recv()
-    swap = begin(rcopy(whole.at[pl.ds(mine, rows)], whole.at[pl.ds(mine, rows)], core_send.at[1], core_recv.at[1], other))
+        for s in range(2):
+            copies[s].wait_recv()
+            passed.append(to_other(5 - k, s, offs[s] + (1 - 2 * steps[s][k][1]) * size, size))
     poll(4)
     accumulate(4)
-    swap.wait_recv()
+    for copy in passed:
+        copy.wait_recv()
 
     wlen = mixed.shape[0] // 2
     woffs = dp_offsets(dp, core, wlen)
@@ -300,14 +395,13 @@
 
     mixed_send(0)
 
-    at = 0
     for i in range(nblk):
         for j in range(nblk):
             if j < i:
-                inv_ref[i * NB : (i + 1) * NB, j * NB : (j + 1) * NB] = jnp.zeros((NB, NB), F32)
+                value = jnp.zeros((NB, NB), F32)
             else:
-                inv_ref[i * NB : (i + 1) * NB, j * NB : (j + 1) * NB] = whole[at : at + NB, :]
-                at += NB
+                value = whole[spots[i, j] : spots[i, j] + NB, :]
+            inv_ref[i * NB : (i + 1) * NB, j * NB : (j + 1) * NB] = value
 
     def between(k):
         for phase in range(3):
@@ -316,137 +410,48 @@
                 mixed_add(phase)
                 mixed_send(phase + 1)
 
-    chol_inv(inv_ref, block, between)
-
-    mixed_add(3)
-    size = wlen >> 4
-    for s in range(2):
-        mixed_ref[s * size : (s + 1) * size, :] = mixed[pl.ds(pl.multiple_of(s * wlen + woffs[s], 8), size), :]
-    for k in range(4):
-        for s in range(2):
-            mixed_copy(k, s)[0].wait_send()
-    for copy in pending:
-        copy.wait_send()
-
-
-def factor(projected, buffer):
-    prows, n = projected.shape
-    depth = buffer.shape[1]
-    nblk = n // NB
-    packed = nblk * (nblk + 1) // 2 * NB
-    nz = lax.axis_size("tensor") // 2
-    ndp = lax.axis_size("dp")
-    rows = packed // 2
-    last = rows // 2 // 16
-    piece = -(-2 * last // (8 * nz)) * 8
-    dma = pltpu.SemaphoreType.DMA
-    vmem = pl.BlockSpec(memory_space=pltpu.VMEM)
-    return pl.pallas_call(
-        factor_kernel,
-        out_shape=[
-            jax.ShapeDtypeStruct((n, n), F32),
-            jax.ShapeDtypeStruct((depth // ndp, n), F32),
-            jax.ShapeDtypeStruct((prows * 2 * nz, n), F32),
-        ],
-        in_specs=[vmem] * 2,
-        out_specs=[vmem] * 3,
-        scratch_shapes=[
-            pltpu.VMEM((packed, NB), F32),
-            pltpu.VMEM((rows, NB), F32),
-            pltpu.VMEM((2, rows // 2, NB), F32),
-            pltpu.VMEM((piece * nz, NB), F32),
-            pltpu.VMEM((nz, piece, NB), F32),
-            pltpu.VMEM((piece * nz, NB), F32),
-            pltpu.VMEM((packed, NB), F32),
-            pltpu.VMEM((NB, NB), F32),
-            pltpu.VMEM((depth, n), F32),
-            pltpu.VMEM((2, depth // 2, n), F32),
-            dma((2,)), dma((2,)), dma((2, 4)), dma((2, 4)), dma((nz,)), dma((nz,)),
-            dma((2, 4)), dma((2, 4)), dma((nz,)), dma((nz,)),
-            dma((nz // 2,)), dma((nz // 2,)), dma((nz // 2,)), dma((nz // 2,)), dma((nz,)), dma((nz,)),
-            dma((2, 4)), dma((2, 4)),
-        ],
-        compiler_params=pltpu.CompilerParams(
-            vmem_limit_bytes=56 << 20, collective_id=1, has_side_effects=True
-        ),
-        cost_estimate=pl.CostEstimate(flops=60_000_000_000, bytes_accessed=24 << 20, transcendentals=0),
-        name="factor",
-    )(projected, buffer)
-
-
-def dp_offsets(dp, core, length):
-    def bits(v):
-        gray, high = lax.rem(v + v // 2, 2), v // 2
-        other = 1 - core
-        return [other * gray + core * high, other * high + core * gray]
-
-    xs, ys = bits(lax.rem(dp, 4)), bits(dp // 4)
-    out = []
-    for order in (xs + ys, ys + xs):
-        at, size = 0, length
-        for bit in order:
-            size //= 2
-            at = at + bit * size
-        out.append(at)
-    return out
-
-
-def finish_kernel(mixed_ref, inv_ref, proj_ref, ortho_ref, trans_ref, basis_ref, inv_hi, inv_lo, stacked, whole, sq, sq_t, sq_d, sq_sum, ag_send, ag_recv, t_send, t_recv, d_send, d_recv):
-    dp, tensor = lax.axis_index("dp"), lax.axis_index("tensor")
-    ndp, ntensor = lax.axis_size("dp"), lax.axis_size("tensor")
-    core = lax.rem(tensor, 2)
-    steps = dp_steps(core)
-    tdev = [(dp, lax.rem(tensor + d, ntensor)) for d in range(ntensor)]
-    ddev = [(lax.rem(dp + d, ndp), tensor) for d in range(ndp)]
-    enter(tdev[1:] + ddev[1:])
-
-    n = inv_ref.shape[0]
+    chol_inv(inv_ref, block, left, right, between)
+
     for k in range(0, n, 256):
         wide = inv_ref[k : k + 256, :]
         high = wide.astype(BF16)
         inv_hi[k : k + 256, :] = high
         inv_lo[k : k + 256, :] = (wide - high.astype(F32)).astype(BF16)
-    share = mixed_ref.shape[0]
-    high = mixed_ref[...].astype(BF16)
-    stacked[0:share, :] = high
-    stacked[share:, :] = (mixed_ref[...] - high.astype(F32)).astype(BF16)
-    length = whole.shape[0] // 2
-    offs = dp_offsets(dp, core, length)
-    spots = [pl.multiple_of(s * length + offs[s], 16) for s in range(2)]
+    mixed_add(3)
+    piece = wlen >> 4
+    share = 2 * piece
+    rows_at = [pl.multiple_of(s * wlen + woffs[s], 16) for s in range(2)]
+    for s in range(2):
+        wide = mixed[pl.ds(rows_at[s], piece), :]
+        high = wide.astype(BF16)
+        stacked[s * piece : (s + 1) * piece, :] = high
+        stacked[share + s * piece : share + (s + 1) * piece, :] = (wide - high.astype(F32)).astype(BF16)
     for k in range(0, n, 256):
         both = mm_nt(stacked[...], inv_hi[k : k + 256, :])
-        part = both[0:share, :] + both[share:, :] + mm_nt(stacked[0:share, :], inv_lo[k : k + 256, :])
-        squares = jnp.sum(part * part, axis=0, keepdims=True)
+        trans = both[0:share, :] + both[share:, :] + mm_nt(stacked[0:share, :], inv_lo[k : k + 256, :])
+        squares = jnp.sum(trans * trans, axis=0, keepdims=True)
         for j in range(0, 256, NB):
             sq[(k + j) // NB : (k + j) // NB + 1, :] = squares[:, j : j + NB]
-        part = part.astype(BF16)
-        for s in range(2):
-            whole[pl.ds(spots[s], share // 2), k : k + 256] = part[s * share // 2 : (s + 1) * share // 2, :]
-
-    pending = []
+        half_part = trans.astype(BF16)
+        for s in range(2):
+            trans_ref[pl.ds(rows_at[s], piece), k : k + 256] = half_part[s * piece : (s + 1) * piece, :]
 
     def gather_step(k):
-        size = length >> (k + 1)
+        size = wlen >> (k + 1)
         copies = []
         for s in range(2):
-            start = s * length + offs[s] // size * size
-            region = whole.at[pl.ds(pl.multiple_of(start, 16), size)]
-            copy = rcopy(region, region, ag_send.at[s, k], ag_recv.at[s, k], (steps[s][k][0], tensor))
-            copy.start()
-            copies.append(copy)
-        pending.extend(copies)
+            start = s * wlen + woffs[s] // size * size
+            here = trans_ref.at[pl.ds(pl.multiple_of(start, 16), size)]
+            copies.append(begin(rcopy(here, here, tr_send.at[s, k], tr_recv.at[s, k], (steps[s][k][0], tensor))))
         return copies
 
     def spread(source, slots, send, recv, devices):
         copies = []
         for d in range(1, len(devices)):
-            copy = rcopy(source, slots.at[d], send.at[d], recv.at[d], devices[d])
-            copy.start()
-            copies.append(copy)
-        pending.extend(copies)
+            copies.append(begin(rcopy(source, slots.at[d], send.at[d], recv.at[d], devices[d])))
         return copies
 
-    def total(source, slots, copies):
+    def sum_of(source, slots, copies):
         out = source[...]
         for d in range(1, slots.shape[0]):
             copies[d - 1].wait_recv()
@@ -454,69 +459,88 @@
         return out
 
     def ortho_part(i):
-        rows = proj_ref.shape[0] // 4
-        rows0 = i * rows
-        wide = proj_ref[rows0 : rows0 + rows, :]
+        count = all_ref.shape[0] // 4
+        rows0 = i * count
+        wide = all_ref[rows0 : rows0 + count, :]
         high = wide.astype(BF16)
         low = (wide - high.astype(F32)).astype(BF16)
         for k in range(0, n, 256):
             e = k + 256
             hi, lo = inv_hi[k:e, 0:e], inv_lo[k:e, 0:e]
             value = mm_nt(high[:, 0:e], hi) + (mm_nt(low[:, 0:e], hi) + mm_nt(high[:, 0:e], lo))
-            ortho_ref[rows0 : rows0 + rows, k:e] = value.astype(BF16)
-
-    across = spread(sq, sq_t, t_send, t_recv, tdev)
+            ortho_ref[rows0 : rows0 + count, k:e] = value.astype(BF16)
+
+    beside = spread(sq, sq_t, t_send, t_recv, tdev)
     copies = gather_step(3)
     ortho_part(0)
-    sq_sum[...] = total(sq, sq_t, across)
+    sq_sum[...] = sum_of(sq, sq_t, beside)
     down = spread(sq_sum, sq_d, d_send, d_recv, ddev)
     for i, k in enumerate((2, 1, 0)):
         for copy in copies:
             copy.wait_recv()
         copies = gather_step(k)
         ortho_part(i + 1)
-    scale = lax.rsqrt(total(sq_sum, sq_d, down) + NORM_EPS)
+    scale = lax.rsqrt(sum_of(sq_sum, sq_d, down) + NORM_EPS)
     for copy in copies:
         copy.wait_recv()
-    for rows0 in range(0, whole.shape[0], NB):
-        block = whole[rows0 : rows0 + NB, :]
-        trans_ref[rows0 : rows0 + NB, :] = block
+    for rows0 in range(0, trans_ref.shape[0], NB):
         for j in range(n // NB):
-            basis_ref[rows0 : rows0 + NB, j * NB : (j + 1) * NB] = (
-                block[:, j * NB : (j + 1) * NB].astype(F32) * scale[j : j + 1, :]
-            ).astype(BF16)
+            value = trans_ref[rows0 : rows0 + NB, j * NB : (j + 1) * NB].astype(F32)
+            basis_ref[rows0 : rows0 + NB, j * NB : (j + 1) * NB] = (value * scale[j : j + 1, :]).astype(BF16)
+    for k in range(4):
+        for s in range(2):
+            mixed_copy(k, s)[0].wait_send()
     for copy in pending:
         copy.wait_send()
 
 
-def finish(mixed, inverse, proj_all):
-    share, n = mixed.shape
-    rows = proj_all.shape[0]
-    ndp, ntensor = lax.axis_size("dp"), lax.axis_size("tensor")
+def factor(projected, buffer):
+    prows, n = projected.shape
+    depth = buffer.shape[1]
+    nblk = n // NB
+    packed = nblk * (nblk + 1) // 2 * NB
+    ntensor, ndp = lax.axis_size("tensor"), lax.axis_size("dp")
+    nz = ntensor // 2
+    rows = packed // 2
+    last = rows // 2 // 16
+    piece = -(-2 * last // (8 * nz)) * 8
     dma = pltpu.SemaphoreType.DMA
     vmem = pl.BlockSpec(memory_space=pltpu.VMEM)
+
+    def f32(*shape):
+        return pltpu.VMEM(shape, F32)
+
+    def bf16(*shape):
+        return pltpu.VMEM(shape, BF16)
+
     return pl.pallas_call(
-        finish_kernel,
+        factor_kernel,
         out_shape=[
-            jax.ShapeDtypeStruct((rows, n), BF16),
-            jax.ShapeDtypeStruct((share * ndp, n), BF16),
-            jax.ShapeDtypeStruct((share * ndp, n), BF16),
+            jax.ShapeDtypeStruct((prows * ntensor, n), BF16),
+            jax.ShapeDtypeStruct((depth, n), BF16),
+            jax.ShapeDtypeStruct((depth, n), BF16),
         ],
-        in_specs=[vmem] * 3,
+        in_specs=[vmem] * 2,
         out_specs=[vmem] * 3,
         scratch_shapes=[
-            pltpu.VMEM((n, n), BF16), pltpu.VMEM((n, n), BF16),
-            pltpu.VMEM((2 * share, n), BF16), pltpu.VMEM((share * ndp, n), BF16),
-            pltpu.VMEM((n // NB, NB), F32), pltpu.VMEM((ntensor, n // NB, NB), F32),
-            pltpu.VMEM((ndp, n // NB, NB), F32), pltpu.VMEM((n // NB, NB), F32),
-            dma((2, 4)), dma((2, 4)), dma((ntensor,)), dma((ntensor,)), dma((ndp,)), dma((ndp,)),
+            f32(n, n), f32(prows * ntensor, n), bf16(6 * NB, n), bf16(6 * NB, n),
+            bf16(n, n), bf16(n, n), bf16(2 * depth // ndp, n),
+            f32(packed, NB), f32(rows, NB), f32(2, rows // 2, NB),
+            f32(piece * nz, NB), f32(nz, piece, NB), f32(piece * nz, NB), f32(packed, NB),
+            f32(NB, NB), f32(depth, n), f32(2, depth // 2, n),
+            f32(nblk, NB), f32(ntensor, nblk, NB), f32(ndp, nblk, NB), f32(nblk, NB),
+            dma((2, 6)), dma((2, 6)), dma((2, 4)), dma((2, 4)), dma((nz,)), dma((nz,)),
+            dma((2, 4)), dma((2, 4)), dma((nz,)), dma((nz,)),
+            dma((nz // 2,)), dma((nz // 2,)), dma((nz // 2,)), dma((nz // 2,)), dma((nz,)), dma((nz,)),
+            dma((2, 4)), dma((2, 4)), dma((2, 4)), dma((2, 4)),
+            dma((ntensor,)), dma((ntensor,)), dma((ndp,)), dma((ndp,)),
         ],
         compiler_params=pltpu.CompilerParams(
-            vmem_limit_bytes=48 << 20, collective_id=2, has_side_effects=True
+            vmem_limit_bytes=58 << 20, collective_id=1, has_side_effects=True
         ),
-        cost_estimate=pl.CostEstimate(flops=20_000_000_000, bytes_accessed=16 << 20, transcendentals=0),
-        name="finish",
-    )(mixed, inverse, proj_all)
+        cost_estimate=pl.CostEstimate(flops=60_000_000_000, bytes_accessed=24 << 20, transcendentals=0),
+        name="factor",
+    )(projected, buffer)
 
 
 def project_kernel(buf_ref, share_ref, out_ref, basis, natural, part, swapped, acc, ring, ag_send, ag_recv, sw_send, sw_recv, ring_send, ring_recv):
@@ -642,8 +666,7 @@
     share = old_basis.shape[1]
     rank = share * lax.axis_size("dp")
     projected = project(buffer, old_basis.T)
-    inverse, mixed, proj_all = factor(projected, buffer)
-    ortho_all, trans_all, basis_all = finish(mixed, inverse, proj_all)
+    ortho_all, trans_all, basis_all = factor(projected, buffer)
     new_basis = lax.dynamic_slice_in_dim(basis_all, lax.axis_index("dp") * share, share, axis=1)
     feedback = mm_nt(ortho_all, trans_all)
     new_buffer = (buffer.astype(F32) - FEEDBACK_SHARE * feedback).astype(BF16)

time: 258 us -> 234 us (0.907)
  Pallas kernels: 239 us -> 215 us
    pallas_call x2 -> x1, Pallas kernels: 170 us -> 146 us  [factor(): pl.pallas_call(factor_kernel, out_shape=[jax.ShapeDtypeStruct((prows * nt...]
where the time goes in v4:
time: 234 us
  Pallas kernels  215 us (92%)
  matrix products  13.9 us (6%)
  local copies, waits for them, and re-layouts  4.56 us (2%)
    pallas_call x1, Pallas kernels, factor(): pl.pallas_call(factor_kernel, out_shape=[jax.ShapeDtypeStruct((prows * nt...  146 us
    pallas_call x1, Pallas kernels, project(): pl.pallas_call(project_kernel, out_shape=jax.ShapeDtypeStruct((rows, n),...  68.8 us
    dot_general x2, matrix products, mm_nt(): lax.dot_general(a, b, (((1,), (1,)), ((), ())), precision=precision, pref...  13.9 us

profile of v4, /device:TPU:1, one launch (start us, length us, event | category | flops | bytes accessed | tf_op | source)
XLA Modules:
  0.0 234.3 jit_solution(14910695190370772689)
XLA Ops:
  0.6 0.0 copy-start
  0.6 2.0 copy-done
  2.6 0.0 copy-start.2
  2.6 0.9 copy-done.2
  3.5 68.8 %project.1.p_ref = f32[104,1024]{1,0:T(8,128)S(1)} custom-call(bf16[1664,1024]{1,0:T(8,128)(2,1)S(1)} %copy-done, bf16[64,1024]{1,0:T(8,128)(2,1)S(1)} %bitcast.5), custom_call_target="tpu_custom_call" | custom-call | flops 20000000000 | bytes 16777216 | tf_op jit(solution)/shard_map/project/pallas_call | solution.py:645
  72.3 0.0 copy-start.3
  72.3 0.7 copy-done.3
  73.0 0.0 copy-start.1
  73.0 146.3 %factor.1 = (bf16[1664,1024]{1,0:T(8,128)(2,1)}, bf16[1024,1024]{1,0:T(8,128)(2,1)}, bf16[1024,1024]{1,0:T(8,128)(2,1)}) custom-call(f32[104,1024]{1,0:T(8,128)} %copy-done.3, bf16[1664,1024]{1,0:T(8,128)(2,1)} %buf_ref.3), custom_call_target="tpu_custom_call" | custom-call | flops 60000002048 | bytes 25165824 | tf_op jit(solution)/shard_map/factor/pallas_call | solution.py:516
  219.4 0.0 copy-done.1
  219.4 0.0 copy-start.4
  219.4 0.0 copy-start.5
  219.4 8.7 %subtract_convert_fusion = bf16[1664,1024]{1,0:T(8,128)(2,1)} fusion(bf16[1664,1024]{1,0:T(8,128)(2,1)S(1)} %copy-done.1, bf16[1664,1024]{1,0:T(8,128)(2,1)} %get-tuple-element.6, bf16[1024,1024]{1,0:T(8,128)(2,1)} %get-tuple-element.7), kind=kOutput, calls=%fused_computation.1 | convolution fusion | flops 3496476672 | bytes 12320768 | tf_op jit(solution)/shard_map/dot_general | solution.py:32
  228.1 0.0 copy-done.4
  228.1 0.0 copy-done.5
  228.1 5.2 %multiply_convert_fusion = bf16[1664,1024]{1,0:T(8,128)(2,1)} fusion(bf16[1664,1024]{1,0:T(8,128)(2,1)S(1)} %copy-done.5, bf16[1024,1024]{1,0:T(8,128)(2,1)S(1)} %copy-done.4), kind=kOutput, calls=%fused_computation | convolution fusion | flops 3493068800 | bytes 8912896 | tf_op jit(solution)/shard_map/dot_general | solution.py:32
  233.3 0.1 constant_dynamic-slice_fusion
  233.5 0.8 copy.5
Async XLA Ops:
  0.6 2.0 copy-start
  2.6 0.9 copy-start.2
  72.3 0.8 copy-start.3
  73.0 146.3 %copy-start.1 = (bf16[1664,1024]{1,0:T(8,128)(2,1)S(1)}, bf16[1664,1024]{1,0:T(8,128)(2,1)}, u32[]{:S(2)}) copy-start(bf16[1664,1024]{1,0:T(8,128)(2,1)} %buf_ref.3) | copy-start | bytes 10223620
  219.4 8.7 %copy-start.4 = (bf16[1024,1024]{1,0:T(8,128)(2,1)S(1)}, bf16[1024,1024]{1,0:T(8,128)(2,1)}, u32[]{:S(2)}) copy-start(bf16[1024,1024]{1,0:T(8,128)(2,1)} %get-tuple-element.8) | copy-start | bytes 6291460
  219.4 8.7 %copy-start.5 = (bf16[1664,1024]{1,0:T(8,128)(2,1)S(1)}, bf16[1664,1024]{1,0:T(8,128)(2,1)}, u32[]{:S(2)}) copy-start(bf16[1664,1024]{1,0:T(8,128)(2,1)} %get-tuple-element.6) | copy-start | bytes 10223620

commit v5 on v4

--- a/solution.py
+++ b/solution.py
@@ -1,3 +1,4 @@
+import functools
 import math
 
 import jax
@@ -170,11 +171,11 @@
 
 def dp_offsets(dp, core, length):
     def bits(v):
-        gray, high = lax.rem(v + v // 2, 2), v // 2
+        gray, high = (v + v // 2) % 2, v // 2
         other = 1 - core
         return [other * gray + core * high, other * high + core * gray]
 
-    xs, ys = bits(lax.rem(dp, 4)), bits(dp // 4)
+    xs, ys = bits(dp % 4), bits(dp // 4)
     out = []
     for order in (xs + ys, ys + xs):
         at, size = 0, length
@@ -202,9 +203,13 @@
 
     prows, n = p_ref.shape
 
-    def region(r, c):
-        at = (lax.rem(z + r, nz) * 2 + c) * prows
-        return all_ref.at[pl.ds(pl.multiple_of(at, 8), prows)]
+    places = [lax.rem(z + (1 - 2 * core) * r + nz, nz) for r in range(nz)]
+    ahead, behind = [(dp, places[r] * 2 + core) for r in (1, nz - 1)]
+
+    own_at = [pl.multiple_of((places[r] * 2 + core) * prows, 8) for r in range(nz)]
+
+    def region(r):
+        return all_ref.at[pl.ds(own_at[r], prows)]
 
     def begin(copy):
         copy.start()
@@ -212,47 +217,47 @@
         return copy
 
     def pass_on(j):
-        plus = region(nz - j if j else 0, core)
-        begin(rcopy(plus, plus, plus_send.at[j], plus_recv.at[j], zdev[1]))
+        plus = region(nz - j if j else 0)
+        begin(rcopy(plus, plus, plus_send.at[j], plus_recv.at[j], ahead))
         if j < nz // 2 - 1:
-            minus = region(j, core)
-            begin(rcopy(minus, minus, minus_send.at[j], minus_recv.at[j], zdev[nz - 1]))
+            minus = region(j)
+            begin(rcopy(minus, minus, minus_send.at[j], minus_recv.at[j], behind))
+
+    def pair_copy(r):
+        here = region(r)
+        return rcopy(here, here, pair_send.at[r], pair_recv.at[r], other)
 
     def across(r):
-        here = region(r, core)
-        begin(rcopy(here, here, pair_send.at[r], pair_recv.at[r], other))
+        pair_copy(r).start()
 
     def poll(j):
-        here = region(nz - j, core)
-        rcopy(here, here, plus_send.at[j - 1], plus_recv.at[j - 1], zdev[1]).wait_recv()
+        here = region(nz - j)
+        rcopy(here, here, plus_send.at[j - 1], plus_recv.at[j - 1], ahead).wait_recv()
         if j < nz // 2:
-            here = region(j, core)
-            rcopy(here, here, minus_send.at[j - 1], minus_recv.at[j - 1], zdev[nz - 1]).wait_recv()
+            here = region(j)
+            rcopy(here, here, minus_send.at[j - 1], minus_recv.at[j - 1], behind).wait_recv()
             pass_on(j)
             across(j)
         across(nz - j)
 
     chunk = 2 * prows
+    chunk_at = [pl.multiple_of(places[r] * chunk, 16) for r in range(nz)]
 
     def accumulate(r):
-        here = region(r, core)
-        rcopy(here, here, pair_send.at[r], pair_recv.at[r], other).wait_recv()
-        rows0 = pl.multiple_of(lax.rem(z + r, nz) * chunk, 16)
+        here = region(r)
+        rcopy(here, here, pair_send.at[r], pair_recv.at[(nz - r) % nz], other).wait_recv()
+        rows0 = chunk_at[r]
         wide = all_ref[pl.ds(rows0, chunk), :]
         high = wide.astype(BF16)
         low = (wide - high.astype(F32)).astype(BF16)
 
-        def strip(i, _):
-            i0 = pl.multiple_of(i * 256, 256)
-            left = buf_ref[pl.ds(rows0, chunk), pl.ds(i0, 256)]
+        for i0 in range(0, mixed.shape[0], 256):
+            columns = buf_ref[pl.ds(rows0, chunk), i0 : i0 + 256]
             for k in range(0, n, 256):
-                value = mm_tn(left, high[:, k : k + 256]) + mm_tn(left, low[:, k : k + 256])
+                value = mm_tn(columns, high[:, k : k + 256]) + mm_tn(columns, low[:, k : k + 256])
                 if r:
-                    value = value + mixed[pl.ds(i0, 256), k : k + 256]
-                mixed[pl.ds(i0, 256), k : k + 256] = value
-            return 0
-
-        lax.fori_loop(0, mixed.shape[0] // 256, strip, 0)
+                    value = value + mixed[i0 : i0 + 256, k : k + 256]
+                mixed[i0 : i0 + 256, k : k + 256] = value
 
     own_rows = pl.multiple_of(tensor * prows, 8)
     all_ref[pl.ds(own_rows, prows), :] = p_ref[...]
@@ -299,7 +304,7 @@
     half[...] = half[...] + part[pl.ds(mine, rows), :]
 
     length = rows // 2
-    offs = [jnp.int32(0), jnp.int32(length)]
+    offs = [0, length]
     trail = []
     size = length
     got_at = 0
@@ -314,8 +319,6 @@
             offs[s] = keep
         if k == 0:
             accumulate(0)
-        elif k >= 2:
-            accumulate((1, nz - 1)[k - 2])
         for s in range(2):
             copies[s].wait_recv()
             half[pl.ds(offs[s], size), :] = half[pl.ds(offs[s], size), :] + got[s, pl.ds(got_at, size), :]
@@ -333,7 +336,6 @@
     for d in range(1, nz):
         zto = lax.rem(z + d, nz)
         copies.append(begin(rcopy(sums.at[pl.ds(pl.multiple_of(zto * piece, 8), piece)], zgot.at[d], z_send.at[d], z_recv.at[d], zdev[d])))
-    poll(2)
     own = pl.multiple_of(z * piece, 8)
     total = sums[pl.ds(own, piece), :]
     for d in range(1, nz):
@@ -345,6 +347,7 @@
         copies.append(begin(rcopy(zsums.at[pl.ds(own, piece)], zsums.at[pl.ds(own, piece)], zag_send.at[d], zag_recv.at[d], zdev[d])))
     for copy in copies:
         copy.wait_recv()
+    poll(2)
 
     def to_other(stage, s, start, count):
         here = whole.at[pl.ds(pl.multiple_of(mine + start, 8), count)]
@@ -360,14 +363,17 @@
         for s in range(2):
             here = whole.at[pl.ds(pl.multiple_of(mine + offs[s], 8), size)]
             copies.append(begin(rcopy(here, here, ag_send.at[s, k], ag_recv.at[s, k], (steps[s][k][0], tensor))))
-        if k == 2:
+        if k == 3:
+            accumulate(1)
+        elif k == 2:
+            accumulate(nz - 1)
+        elif k == 0:
             poll(3)
-        accumulate((nz - 3, 3, nz - 2, 2)[k])
+            accumulate(2)
+            accumulate(nz - 2)
         for s in range(2):
             copies[s].wait_recv()
             passed.append(to_other(5 - k, s, offs[s] + (1 - 2 * steps[s][k][1]) * size, size))
-    poll(4)
-    accumulate(4)
     for copy in passed:
         copy.wait_recv()
 
@@ -393,8 +399,6 @@
         for s in range(2):
             mixed_copy(k, s)[0].start()
 
-    mixed_send(0)
-
     for i in range(nblk):
         for j in range(nblk):
             if j < i:
@@ -404,8 +408,19 @@
             inv_ref[i * NB : (i + 1) * NB, j * NB : (j + 1) * NB] = value
 
     def between(k):
-        for phase in range(3):
-            @pl.when(k == phase + 2)
+        @pl.when(k == 0)
+        def _():
+            accumulate(3)
+            accumulate(nz - 3)
+
+        @pl.when(k == 1)
+        def _():
+            poll(nz // 2)
+            accumulate(nz // 2)
+            mixed_send(0)
+
+        for phase, at in enumerate((4, 6, 7)):
+            @pl.when(k == at)
             def _():
                 mixed_add(phase)
                 mixed_send(phase + 1)
@@ -413,10 +428,10 @@
     chol_inv(inv_ref, block, left, right, between)
 
     for k in range(0, n, 256):
-        wide = inv_ref[k : k + 256, :]
+        wide = inv_ref[k : k + 256, 0 : k + 256]
         high = wide.astype(BF16)
-        inv_hi[k : k + 256, :] = high
-        inv_lo[k : k + 256, :] = (wide - high.astype(F32)).astype(BF16)
+        inv_hi[k : k + 256, 0 : k + 256] = high
+        inv_lo[k : k + 256, 0 : k + 256] = (wide - high.astype(F32)).astype(BF16)
     mixed_add(3)
     piece = wlen >> 4
     share = 2 * piece
@@ -426,23 +441,24 @@
         high = wide.astype(BF16)
         stacked[s * piece : (s + 1) * piece, :] = high
         stacked[share + s * piece : share + (s + 1) * piece, :] = (wide - high.astype(F32)).astype(BF16)
-    for k in range(0, n, 256):
-        both = mm_nt(stacked[...], inv_hi[k : k + 256, :])
-        trans = both[0:share, :] + both[share:, :] + mm_nt(stacked[0:share, :], inv_lo[k : k + 256, :])
+    def trans_part(k):
+        e = k + 256
+        both = mm_nt(stacked[:, 0:e], inv_hi[k:e, 0:e])
+        trans = both[0:share, :] + both[share:, :] + mm_nt(stacked[0:share, 0:e], inv_lo[k:e, 0:e])
         squares = jnp.sum(trans * trans, axis=0, keepdims=True)
         for j in range(0, 256, NB):
             sq[(k + j) // NB : (k + j) // NB + 1, :] = squares[:, j : j + NB]
         half_part = trans.astype(BF16)
         for s in range(2):
-            trans_ref[pl.ds(rows_at[s], piece), k : k + 256] = half_part[s * piece : (s + 1) * piece, :]
-
-    def gather_step(k):
+            trans_ref[pl.ds(rows_at[s], piece), k:e] = half_part[s * piece : (s + 1) * piece, :]
+
+    def gather_step(q, k):
         size = wlen >> (k + 1)
         copies = []
         for s in range(2):
             start = s * wlen + woffs[s] // size * size
-            here = trans_ref.at[pl.ds(pl.multiple_of(start, 16), size)]
-            copies.append(begin(rcopy(here, here, tr_send.at[s, k], tr_recv.at[s, k], (steps[s][k][0], tensor))))
+            here = trans_ref.at[pl.ds(pl.multiple_of(start, 16), size), pl.ds(q * n // 2, n // 2)]
+            copies.append(begin(rcopy(here, here, tr_send.at[q, s, k], tr_recv.at[q, s, k], (steps[s][k][0], tensor))))
         return copies
 
     def spread(source, slots, send, recv, devices):
@@ -470,18 +486,25 @@
             value = mm_nt(high[:, 0:e], hi) + (mm_nt(low[:, 0:e], hi) + mm_nt(high[:, 0:e], lo))
             ortho_ref[rows0 : rows0 + count, k:e] = value.astype(BF16)
 
+    trans_part(0)
+    trans_part(256)
+    coming = [gather_step(0, 3)]
+    trans_part(512)
+    trans_part(768)
+    coming.append(gather_step(1, 3))
     beside = spread(sq, sq_t, t_send, t_recv, tdev)
-    copies = gather_step(3)
-    ortho_part(0)
-    sq_sum[...] = sum_of(sq, sq_t, beside)
-    down = spread(sq_sum, sq_d, d_send, d_recv, ddev)
     for i, k in enumerate((2, 1, 0)):
-        for copy in copies:
-            copy.wait_recv()
-        copies = gather_step(k)
-        ortho_part(i + 1)
+        ortho_part(i)
+        for q in range(2):
+            for copy in coming[q]:
+                copy.wait_recv()
+            coming[q] = gather_step(q, k)
+        if i == 0:
+            sq_sum[...] = sum_of(sq, sq_t, beside)
+            down = spread(sq_sum, sq_d, d_send, d_recv, ddev)
+    ortho_part(3)
     scale = lax.rsqrt(sum_of(sq_sum, sq_d, down) + NORM_EPS)
-    for copy in copies:
+    for copy in coming[0] + coming[1]:
         copy.wait_recv()
     for rows0 in range(0, trans_ref.shape[0], NB):
         for j in range(n // NB):
@@ -490,6 +513,8 @@
     for k in range(4):
         for s in range(2):
             mixed_copy(k, s)[0].wait_send()
+    for r in range(nz):
+        pair_copy(r).wait_send()
     for copy in pending:
         copy.wait_send()
 
@@ -532,7 +557,7 @@
             dma((2, 6)), dma((2, 6)), dma((2, 4)), dma((2, 4)), dma((nz,)), dma((nz,)),
             dma((2, 4)), dma((2, 4)), dma((nz,)), dma((nz,)),
             dma((nz // 2,)), dma((nz // 2,)), dma((nz // 2,)), dma((nz // 2,)), dma((nz,)), dma((nz,)),
-            dma((2, 4)), dma((2, 4)), dma((2, 4)), dma((2, 4)),
+            dma((2, 4)), dma((2, 4)), dma((2, 2, 4)), dma((2, 2, 4)),
             dma((ntensor,)), dma((ntensor,)), dma((ndp,)), dma((ndp,)),
         ],
         compiler_params=pltpu.CompilerParams(
@@ -554,83 +579,110 @@
     enter([(partner, tensor) for partner, _ in steps[0]] + [other, after, before])
     pending = []
 
-    share = share_ref.shape[0]
-    length = basis.shape[0] // 2
+    def begin(copy):
+        copy.start()
+        pending.append(copy)
+        return copy
+
+    share = share_ref.shape[0] // 2
+    length = basis.shape[1] // 2
     offs = dp_offsets(dp, core, length)
     half = share // 2
-    for s in range(2):
-        basis[pl.ds(pl.multiple_of(s * length + offs[s], 16), half), :] = share_ref[s * half : (s + 1) * half, :]
-    for k in reversed(range(4)):
+    for q in range(2):
+        for s in range(2):
+            basis[q, pl.ds(pl.multiple_of(s * length + offs[s], 16), half), :] = share_ref[
+                q * share + s * half : q * share + (s + 1) * half, :
+            ]
+
+    def gather_step(q, k):
         size = length >> (k + 1)
         copies = []
         for s in range(2):
-            region = basis.at[pl.ds(pl.multiple_of(s * length + offs[s] // size * size, 16), size)]
-            copy = rcopy(region, region, ag_send.at[s, k], ag_recv.at[s, k], (steps[s][k][0], tensor))
-            copy.start()
-            copies.append(copy)
+            here = basis.at[q, pl.ds(pl.multiple_of(s * length + offs[s] // size * size, 16), size)]
+            copies.append(begin(rcopy(here, here, ag_send.at[q, s, k], ag_recv.at[q, s, k], (steps[s][k][0], tensor))))
+        return copies
+
+    def arrive(copies):
         for copy in copies:
             copy.wait_recv()
-        pending += copies
-    for d in range(ndp):
-        there = dp_offsets(jnp.int32(d), core, length)
-        for s in range(2):
-            rows0 = d * share + s * half
-            natural[rows0 : rows0 + half, :] = basis[pl.ds(pl.multiple_of(s * length + there[s], 16), half), :]
+
+    def sort(q):
+        for d in range(ndp):
+            there = dp_offsets(d, core, length)
+            for s in range(2):
+                rows0 = d * share + s * half
+                natural[q, rows0 : rows0 + half, :] = basis[q, pl.ds(pl.multiple_of(s * length + there[s], 16), half), :]
+
+    coming = [gather_step(q, 3) for q in range(2)]
+    for k in (2, 1, 0):
+        for q in range(2):
+            arrive(coming[q])
+            coming[q] = gather_step(q, k)
+    arrive(coming[0])
+    sort(0)
 
     chunk = buf_ref.shape[0] // nz
     rows = chunk // 2
     mine = pl.multiple_of(core * rows, 8)
     theirs = pl.multiple_of((1 - core) * rows, 8)
-
-    def compute(r):
-        rows0 = pl.multiple_of(lax.rem(z + r, nz) * chunk, 16)
-        for k in range(0, natural.shape[0], 512):
-            part[r, :, k : k + 512] = mm_nt(buf_ref[pl.ds(rows0, chunk), :], natural[k : k + 512, :])
-        copy = rcopy(part.at[r, pl.ds(theirs, rows)], swapped.at[r], sw_send.at[r], sw_recv.at[r], other)
-        copy.start()
-        pending.append(copy)
-
     columns = out_ref.shape[1] // 2
 
-    def term(r, h):
-        return part[r, pl.ds(mine, rows), h * columns : (h + 1) * columns] + swapped[r, :, h * columns : (h + 1) * columns]
-
-    def swap_wait(r):
-        rcopy(part.at[r, pl.ds(theirs, rows)], swapped.at[r], sw_send.at[r], sw_recv.at[r], other).wait_recv()
+    def swap(r, q):
+        here = pl.ds(q * columns, columns)
+        return rcopy(part.at[r, pl.ds(theirs, rows), here], swapped.at[r, :, here], sw_send.at[q, r], sw_recv.at[q, r], other)
+
+    def compute(q, *places):
+        for r in places:
+            rows0 = pl.multiple_of(lax.rem(z + r, nz) * chunk, 16)
+            part[r, :, q * columns : (q + 1) * columns] = mm_nt(buf_ref[pl.ds(rows0, chunk), :], natural[q])
+            begin(swap(r, q))
+
+    def term(r, q):
+        here = slice(q * columns, (q + 1) * columns)
+        return part[r, pl.ds(mine, rows), here] + swapped[r, :, here]
 
     last = [None, None]
 
-    def ring_step(s):
+    def ring_step(q, s):
         r = core * (1 + s) + (1 - core) * (nz - 1 - s)
-        swap_wait(r)
-        for h in range(2):
-            value = term(r, h)
-            if s > 0:
-                last[h].wait_recv()
-                value = value + ring[s - 1, h]
-            acc[s, h] = value
-            last[h] = rcopy(acc.at[s, h], ring.at[s, h], ring_send.at[s, h], ring_recv.at[s, h], after)
-            last[h].start()
-            pending.append(last[h])
-
-    order = []
-    for r in range(1, nz // 2):
-        order += [r, nz - r]
-    order += [nz // 2, 0]
-    done = 0
-    for i in range(0, nz, 2):
-        compute(order[i])
-        compute(order[i + 1])
-        if i >= 2:
-            ring_step(done)
-            done += 1
-    for s in range(done, nz - 1):
-        ring_step(s)
-    swap_wait(0)
-    for h in range(2):
-        value = term(0, h)
-        last[h].wait_recv()
-        out_ref[:, h * columns : (h + 1) * columns] = value + ring[nz - 2, h]
+        swap(r, q).wait_recv()
+        value = term(r, q)
+        if s > 0:
+            last[q].wait_recv()
+            value = value + ring[s - 1, q]
+        acc[s, q] = value
+        last[q] = begin(rcopy(acc.at[s, q], ring.at[s, q], ring_send.at[s, q], ring_recv.at[s, q], after))
+
+    pairs = [(r, nz - r) for r in range(1, nz // 2)] + [(nz // 2, 0)]
+    compute(0, *pairs[0])
+    compute(0, *pairs[1])
+    ring_step(0, 0)
+    arrive(coming[1])
+    sort(1)
+    compute(1, *pairs[0])
+    ring_step(0, 1)
+    compute(1, *pairs[1])
+    ring_step(1, 0)
+    for i in range(2, nz // 2):
+        compute(0, *pairs[i])
+        ring_step(0, i)
+        compute(1, *pairs[i])
+        ring_step(1, i - 1)
+    for i in range(nz // 2, nz - 1):
+        ring_step(0, i)
+        ring_step(1, i - 1)
+    ring_step(1, nz - 2)
+    done = []
+    for q in range(2):
+        swap(0, q).wait_recv()
+        value = term(0, q)
+        last[q].wait_recv()
+        done.append(value + ring[nz - 2, q])
+    for j in range(0, 2 * columns, NB):
+        k = j // 2
+        out_ref[:, j : j + NB] = jnp.concatenate(
+            [done[q][:, k + i * share : k + (i + 1) * share] for i in range(NB // 2 // share) for q in range(2)], axis=1
+        )
     for copy in pending:
         copy.wait_send()
 
@@ -648,10 +700,10 @@
         in_specs=[vmem] * 2,
         out_specs=vmem,
         scratch_shapes=[
-            pltpu.VMEM((n, depth), BF16), pltpu.VMEM((n, depth), BF16),
+            pltpu.VMEM((2, n // 2, depth), BF16), pltpu.VMEM((2, n // 2, depth), BF16),
             pltpu.VMEM((nz, 2 * rows, n), F32), pltpu.VMEM((nz, rows, n), F32),
             pltpu.VMEM((nz - 1, 2, rows, n // 2), F32), pltpu.VMEM((nz - 1, 2, rows, n // 2), F32),
-            dma((2, 4)), dma((2, 4)), dma((nz,)), dma((nz,)), dma((nz - 1, 2)), dma((nz - 1, 2)),
+            dma((2, 2, 4)), dma((2, 2, 4)), dma((2, nz)), dma((2, nz)), dma((nz - 1, 2)), dma((nz - 1, 2)),
         ],
         compiler_params=pltpu.CompilerParams(
             vmem_limit_bytes=48 << 20, collective_id=3, has_side_effects=True
@@ -661,6 +713,33 @@
     )(buffer, share)
 
 
+def output_kernel(scale_up, ortho_ref, trans_ref, basis_ref, buf_ref, new_ref, update_ref):
+    ortho = ortho_ref[...]
+    for k in range(0, trans_ref.shape[0], 512):
+        feedback = mm_nt(ortho, trans_ref[k : k + 512, :])
+        new_ref[:, k : k + 512] = (buf_ref[:, k : k + 512].astype(F32) - FEEDBACK_SHARE * feedback).astype(BF16)
+        product = mm_nt(ortho, basis_ref[k : k + 512, :])
+        update_ref[:, k : k + 512] = (-scale_up * product).astype(BF16)
+
+
+def outputs(ortho, trans, basis, buffer, scale_up):
+    rows, depth = buffer.shape
+    n = ortho.shape[1]
+    tile = rows // 4
+    whole = pl.BlockSpec(memory_space=pltpu.VMEM)
+    strip = pl.BlockSpec((tile, depth), lambda i: (i, 0))
+    return pl.pallas_call(
+        functools.partial(output_kernel, scale_up),
+        grid=(rows // tile,),
+        out_shape=[jax.ShapeDtypeStruct((rows, depth), BF16)] * 2,
+        in_specs=[pl.BlockSpec((tile, n), lambda i: (i, 0)), whole, whole, strip],
+        out_specs=[strip, strip],
+        compiler_params=pltpu.CompilerParams(vmem_limit_bytes=40 << 20),
+        cost_estimate=pl.CostEstimate(flops=8_000_000_000, bytes_accessed=20 << 20, transcendentals=0),
+        name="outputs",
+    )(ortho, trans, basis, buffer)
+
+
 def body(buffer, old_basis):
     groups = lax.axis_size("tensor")
     share = old_basis.shape[1]
@@ -668,13 +747,10 @@
     projected = project(buffer, old_basis.T)
     ortho_all, trans_all, basis_all = factor(projected, buffer)
     new_basis = lax.dynamic_slice_in_dim(basis_all, lax.axis_index("dp") * share, share, axis=1)
-    feedback = mm_nt(ortho_all, trans_all)
-    new_buffer = (buffer.astype(F32) - FEEDBACK_SHARE * feedback).astype(BF16)
     scale_up = math.sqrt(
         buffer.shape[0] * lax.axis_size("dp") * buffer.shape[1] * groups / rank
     )
-    product = mm_nt(ortho_all, basis_all)
-    weight_update = (-scale_up * product).astype(BF16)
+    new_buffer, weight_update = outputs(ortho_all, trans_all, basis_all, buffer, scale_up)
     return (new_buffer, weight_update, new_basis)
 
 

time: 234 us -> 228 us (0.974)
  matrix products: 13.9 us -> 0 us
  local copies, waits for them, and re-layouts: 4.56 us -> 10.6 us
    dot_general x2 -> x0, matrix products: 13.9 us -> none  [mm_nt(): lax.dot_general(a, b, (((1,), (1,)), ((), ())), precision=precision, pref...]
    pallas_call x0 -> x1, Pallas kernels: none -> 8.77 us  [outputs(): pl.pallas_call(functools.partial(output_kernel, scale_up), grid=(rows //...]
    pallas_call x1, Pallas kernels: 146 us -> 140 us  [factor(): pl.pallas_call(factor_kernel, out_shape=[jax.ShapeDtypeStruct((prows * nt...]
    unnamed x13 -> x15, local copies, waits for them, and re-layouts: 4.41 us -> 9.54 us
where the time goes in v5:
time: 228 us; the launch traced here: 227 us
  Pallas kernels  216 us (95%)
  local copies, waits for them, and re-layouts  10.6 us (5%)
    pallas_call x1, Pallas kernels, factor(): pl.pallas_call(factor_kernel, out_shape=[jax.ShapeDtypeStruct((prows * nt...  140 us
    pallas_call x1, Pallas kernels, project(): pl.pallas_call(project_kernel, out_shape=jax.ShapeDtypeStruct((rows, n),...  67.8 us
    unnamed x15, local copies, waits for them, and re-layouts  9.54 us
    pallas_call x1, Pallas kernels, outputs(): pl.pallas_call(functools.partial(output_kernel, scale_up), grid=(rows //...  8.77 us

profile of v5, /device:TPU:1, one launch (start us, length us, event | category | flops | bytes accessed | tf_op | source)
XLA Modules:
  0.0 227.5 jit_solution(4406980164220050626)
XLA Ops:
  0.6 0.0 copy-start.1
  0.6 2.0 copy-done.1
  2.6 0.0 copy-start.3
  2.6 0.9 copy-done.3
  3.5 67.8 %project.1.p_ref = f32[104,1024]{1,0:T(8,128)S(1)} custom-call(bf16[1664,1024]{1,0:T(8,128)(2,1)S(1)} %copy-done.1, bf16[64,1024]{1,0:T(8,128)(2,1)S(1)} %bitcast.1), custom_call_target="tpu_custom_call" | custom-call | flops 20000000000 | bytes 16777216 | tf_op jit(solution)/shard_map/project/pallas_call | solution.py:697
  71.3 0.0 copy-start.6
  71.3 0.7 copy-done.6
  72.1 0.0 copy-start.2
  72.1 139.6 %factor.1 = (bf16[1664,1024]{1,0:T(8,128)(2,1)}, bf16[1024,1024]{1,0:T(8,128)(2,1)}, bf16[1024,1024]{1,0:T(8,128)(2,1)}) custom-call(f32[104,1024]{1,0:T(8,128)} %copy-done.6, bf16[1664,1024]{1,0:T(8,128)(2,1)} %buf_ref.5), custom_call_target="tpu_custom_call" | custom-call | flops 60000002048 | bytes 25165824 | tf_op jit(solution)/shard_map/factor/pallas_call | solution.py:541
  211.7 0.0 copy-done.2
  211.7 0.0 copy-start
  211.7 1.6 copy-done
  213.3 0.0 copy-start.4
  213.3 2.0 copy-done.4
  215.3 0.0 copy-start.5
  215.3 1.6 copy-done.5
  216.8 8.8 %outputs.1 = (bf16[1664,1024]{1,0:T(8,128)(2,1)}, bf16[1664,1024]{1,0:T(8,128)(2,1)}) custom-call(bf16[1664,1024]{1,0:T(8,128)(2,1)S(1)} %copy-done.4, bf16[1024,1024]{1,0:T(8,128)(2,1)S(1)} %copy-done.5, bf16[1024,1024]{1,0:T(8,128)(2,1)S(1)} %copy-done, bf16[1664,1024]{1,0:T(8,128)(2,1)S(1)} %copy-done.2), custom_call_target="tpu_custom_call" | custom-call | flops 8000000000 | bytes 20971520 | tf_op jit(solution)/shard_map/outputs/pallas_call | solution.py:731
  225.6 1.1 constant_dynamic-slice_fusion
  226.7 0.8 copy.5
Async XLA Ops:
  0.6 2.0 copy-start.1
  2.6 0.9 copy-start.3
  71.3 0.8 copy-start.6
  72.1 139.6 %copy-start.2 = (bf16[1664,1024]{1,0:T(8,128)(2,1)S(1)}, bf16[1664,1024]{1,0:T(8,128)(2,1)}, u32[]{:S(2)}) copy-start(bf16[1664,1024]{1,0:T(8,128)(2,1)} %buf_ref.5) | copy-start | bytes 10223620
  211.7 1.6 copy-start
  213.3 2.0 copy-start.4
  215.3 1.6 copy-start.5

commit v6 on v5

--- a/solution.py
+++ b/solution.py
@@ -187,7 +187,7 @@
 
 
 def factor_kernel(
-    p_ref, buf_ref, ortho_ref, trans_ref, basis_ref, inv_ref, all_ref, left, right, inv_hi, inv_lo, stacked, part, half, got, sums, zgot, zsums, whole, block, mixed, mixed_got, sq, sq_t, sq_d, sq_sum, core_send, core_recv, dp_send, dp_recv, z_send, z_recv, ag_send, ag_recv, zag_send, zag_recv, plus_send, plus_recv, minus_send, minus_recv, pair_send, pair_recv, w_send, w_recv, tr_send, tr_recv, t_send, t_recv, d_send, d_recv,
+    p_ref, buf_hbm, ortho_hbm, trans_ref, basis_ref, buf_ref, ortho_ref, inv_ref, all_ref, left, right, inv_hi, inv_lo, stacked, part, half, got, sums, zgot, zsums, whole, block, mixed, mixed_got, sq, sq_t, sq_d, sq_sum, core_send, core_recv, dp_send, dp_recv, z_send, z_recv, ag_send, ag_recv, zag_send, zag_recv, plus_send, plus_recv, minus_send, minus_recv, pair_send, pair_recv, w_send, w_recv, tr_send, tr_recv, t_send, t_recv, d_send, d_recv, local_sem,
 ):
     dp, tensor = lax.axis_index("dp"), lax.axis_index("tensor")
     core, z = lax.rem(tensor, 2), tensor // 2
@@ -198,6 +198,8 @@
     zdev = [(dp, lax.rem(z + d, nz) * 2 + core) for d in range(nz)]
     tdev = [(dp, lax.rem(tensor + d, ntensor)) for d in range(ntensor)]
     ddev = [(lax.rem(dp + d, ndp), tensor) for d in range(ndp)]
+    load = pltpu.make_async_copy(buf_hbm, buf_ref, local_sem.at[0])
+    load.start()
     enter(tdev[1:] + ddev[1:])
     pending = []
 
@@ -318,6 +320,7 @@
             copies.append(begin(rcopy(half.at[pl.ds(give, size)], got.at[s, pl.ds(got_at, size)], dp_send.at[s, k], dp_recv.at[s, k], (partner, tensor))))
             offs[s] = keep
         if k == 0:
+            load.wait()
             accumulate(0)
         for s in range(2):
             copies[s].wait_recv()
@@ -474,6 +477,8 @@
             out = out + slots[d]
         return out
 
+    stores = []
+
     def ortho_part(i):
         count = all_ref.shape[0] // 4
         rows0 = i * count
@@ -485,6 +490,10 @@
             hi, lo = inv_hi[k:e, 0:e], inv_lo[k:e, 0:e]
             value = mm_nt(high[:, 0:e], hi) + (mm_nt(low[:, 0:e], hi) + mm_nt(high[:, 0:e], lo))
             ortho_ref[rows0 : rows0 + count, k:e] = value.astype(BF16)
+        here = pl.ds(rows0, count)
+        store = pltpu.make_async_copy(ortho_ref.at[here], ortho_hbm.at[here], local_sem.at[1 + i])
+        store.start()
+        stores.append(store)
 
     trans_part(0)
     trans_part(256)
@@ -513,6 +522,8 @@
     for k in range(4):
         for s in range(2):
             mixed_copy(k, s)[0].wait_send()
+    for store in stores:
+        store.wait()
     for r in range(nz):
         pair_copy(r).wait_send()
     for copy in pending:
@@ -545,10 +556,10 @@
             jax.ShapeDtypeStruct((depth, n), BF16),
             jax.ShapeDtypeStruct((depth, n), BF16),
         ],
-        in_specs=[vmem] * 2,
-        out_specs=[vmem] * 3,
+        in_specs=[vmem, pl.BlockSpec(memory_space=pl.ANY)],
+        out_specs=[pl.BlockSpec(memory_space=pl.ANY), vmem, vmem],
         scratch_shapes=[
-            f32(n, n), f32(prows * ntensor, n), bf16(6 * NB, n), bf16(6 * NB, n),
+            bf16(*buffer.shape), bf16(prows * ntensor, n), f32(n, n), f32(prows * ntensor, n), bf16(6 * NB, n), bf16(6 * NB, n),
             bf16(n, n), bf16(n, n), bf16(2 * depth // ndp, n),
             f32(packed, NB), f32(rows, NB), f32(2, rows // 2, NB),
             f32(piece * nz, NB), f32(nz, piece, NB), f32(piece * nz, NB), f32(packed, NB),
@@ -558,7 +569,7 @@
             dma((2, 4)), dma((2, 4)), dma((nz,)), dma((nz,)),
             dma((nz // 2,)), dma((nz // 2,)), dma((nz // 2,)), dma((nz // 2,)), dma((nz,)), dma((nz,)),
             dma((2, 4)), dma((2, 4)), dma((2, 2, 4)), dma((2, 2, 4)),
-            dma((ntensor,)), dma((ntensor,)), dma((ndp,)), dma((ndp,)),
+            dma((ntensor,)), dma((ntensor,)), dma((ndp,)), dma((ndp,)), dma((5,)),
         ],
         compiler_params=pltpu.CompilerParams(
             vmem_limit_bytes=58 << 20, collective_id=1, has_side_effects=True
@@ -568,7 +579,7 @@
     )(projected, buffer)
 
 
-def project_kernel(buf_ref, share_ref, out_ref, basis, natural, part, swapped, acc, ring, ag_send, ag_recv, sw_send, sw_recv, ring_send, ring_recv):
+def project_kernel(buf_hbm, share_ref, out_ref, buf_ref, basis, natural, part, swapped, acc, ring, load_sem, ag_send, ag_recv, sw_send, sw_recv, ring_send, ring_recv):
     dp, tensor = lax.axis_index("dp"), lax.axis_index("tensor")
     ndp, nz = lax.axis_size("dp"), lax.axis_size("tensor") // 2
     core, z = lax.rem(tensor, 2), tensor // 2
@@ -576,6 +587,8 @@
     after = (dp, lax.rem(z + 1 - 2 * core + nz, nz) * 2 + core)
     before = (dp, lax.rem(z - 1 + 2 * core + nz, nz) * 2 + core)
     steps = dp_steps(core)
+    load = pltpu.make_async_copy(buf_hbm, buf_ref, load_sem.at[0])
+    load.start()
     enter([(partner, tensor) for partner, _ in steps[0]] + [other, after, before])
     pending = []
 
@@ -654,6 +667,7 @@
         last[q] = begin(rcopy(acc.at[s, q], ring.at[s, q], ring_send.at[s, q], ring_recv.at[s, q], after))
 
     pairs = [(r, nz - r) for r in range(1, nz // 2)] + [(nz // 2, 0)]
+    load.wait()
     compute(0, *pairs[0])
     compute(0, *pairs[1])
     ring_step(0, 0)
@@ -697,16 +711,18 @@
     return pl.pallas_call(
         project_kernel,
         out_shape=jax.ShapeDtypeStruct((rows, n), F32),
-        in_specs=[vmem] * 2,
+        in_specs=[pl.BlockSpec(memory_space=pl.ANY), vmem],
         out_specs=vmem,
         scratch_shapes=[
+            pltpu.VMEM(buffer.shape, BF16),
             pltpu.VMEM((2, n // 2, depth), BF16), pltpu.VMEM((2, n // 2, depth), BF16),
             pltpu.VMEM((nz, 2 * rows, n), F32), pltpu.VMEM((nz, rows, n), F32),
             pltpu.VMEM((nz - 1, 2, rows, n // 2), F32), pltpu.VMEM((nz - 1, 2, rows, n // 2), F32),
+            dma((1,)),
             dma((2, 2, 4)), dma((2, 2, 4)), dma((2, nz)), dma((2, nz)), dma((nz - 1, 2)), dma((nz - 1, 2)),
         ],
         compiler_params=pltpu.CompilerParams(
-            vmem_limit_bytes=48 << 20, collective_id=3, has_side_effects=True
+            vmem_limit_bytes=58 << 20, collective_id=3, has_side_effects=True
         ),
         cost_estimate=pl.CostEstimate(flops=20_000_000_000, bytes_accessed=16 << 20, transcendentals=0),
         name="project",
@@ -726,7 +742,7 @@
     rows, depth = buffer.shape
     n = ortho.shape[1]
     tile = rows // 4
-    whole = pl.BlockSpec(memory_space=pltpu.VMEM)
+    whole = pl.BlockSpec((depth, n), lambda i: (0, 0))
     strip = pl.BlockSpec((tile, depth), lambda i: (i, 0))
     return pl.pallas_call(
         functools.partial(output_kernel, scale_up),
@@ -734,7 +750,7 @@
         out_shape=[jax.ShapeDtypeStruct((rows, depth), BF16)] * 2,
         in_specs=[pl.BlockSpec((tile, n), lambda i: (i, 0)), whole, whole, strip],
         out_specs=[strip, strip],
-        compiler_params=pltpu.CompilerParams(vmem_limit_bytes=40 << 20),
+        compiler_params=pltpu.CompilerParams(vmem_limit_bytes=58 << 20),
         cost_estimate=pl.CostEstimate(flops=8_000_000_000, bytes_accessed=20 << 20, transcendentals=0),
         name="outputs",
     )(ortho, trans, basis, buffer)

time: 228 us -> 222 us (0.974)
  local copies, waits for them, and re-layouts: 10.6 us -> 1.87 us
  Pallas kernels: 216 us -> 219 us
    unnamed x15 -> x1, local copies, waits for them, and re-layouts: 9.54 us -> 0.79 us
    pallas_call x1, Pallas kernels: 8.77 us -> 11.6 us  [outputs(): pl.pallas_call(functools.partial(output_kernel, scale_up), grid=(rows //...]
where the time goes in v6:
time: 222 us; the launch traced here: 221 us
  Pallas kernels  219 us (99%)
    pallas_call x1, Pallas kernels, factor(): pl.pallas_call(factor_kernel, out_shape=[jax.ShapeDtypeStruct((prows * nt...  138 us
    pallas_call x1, Pallas kernels, project(): pl.pallas_call(project_kernel, out_shape=jax.ShapeDtypeStruct((rows, n),...  69.7 us
    pallas_call x1, Pallas kernels, outputs(): pl.pallas_call(functools.partial(output_kernel, scale_up), grid=(rows //...  11.6 us

profile of v6, /device:TPU:1, one launch (start us, length us, event | category | flops | bytes accessed | tf_op | source)
XLA Modules:
  0.0 221.3 jit_solution(13272525038142547524)
XLA Ops:
  0.6 69.7 %project.1.p_ref = f32[104,1024]{1,0:T(8,128)} custom-call(bf16[1664,1024]{1,0:T(8,128)(2,1)} %buf_ref.1, bf16[64,1024]{1,0:T(8,128)(2,1)} %bitcast.1), custom_call_target="tpu_custom_call" | custom-call | flops 20000000000 | bytes 16777216 | tf_op jit(solution)/shard_map/project/pallas_call | solution.py:711
  70.3 137.5 %factor.1 = (bf16[1664,1024]{1,0:T(8,128)(2,1)}, bf16[1024,1024]{1,0:T(8,128)(2,1)}, bf16[1024,1024]{1,0:T(8,128)(2,1)}) custom-call(f32[104,1024]{1,0:T(8,128)} %project.1.p_ref, bf16[1664,1024]{1,0:T(8,128)(2,1)} %buf_ref.1), custom_call_target="tpu_custom_call" | custom-call | flops 60000002048 | bytes 25165824 | tf_op jit(solution)/shard_map/factor/pallas_call | solution.py:552
  207.8 11.6 %outputs.1 = (bf16[1664,1024]{1,0:T(8,128)(2,1)}, bf16[1664,1024]{1,0:T(8,128)(2,1)}) custom-call(bf16[1664,1024]{1,0:T(8,128)(2,1)} %get-tuple-element.8.ortho_ref, bf16[1024,1024]{1,0:T(8,128)(2,1)} %get-tuple-element.9.trans_ref, bf16[1024,1024]{1,0:T(8,128)(2,1)} %get-tuple-element.10.basis_ref, bf16[1664,1024]{1,0:T(8,128)(2,1)} %buf_ref.1), custom_call_target="tpu_custom_call" | custom-call | flops 8000000000 | bytes 20971520 | tf_op jit(solution)/shard_map/outputs/pallas_call | solution.py:747
  219.5 1.1 constant_dynamic-slice_fusion
  220.5 0.8 copy.5

commit v7 on v6

--- a/solution.py
+++ b/solution.py
@@ -377,6 +377,8 @@
         for s in range(2):
             copies[s].wait_recv()
             passed.append(to_other(5 - k, s, offs[s] + (1 - 2 * steps[s][k][1]) * size, size))
+    accumulate(3)
+    accumulate(nz - 3)
     for copy in passed:
         copy.wait_recv()
 
@@ -411,11 +413,6 @@
             inv_ref[i * NB : (i + 1) * NB, j * NB : (j + 1) * NB] = value
 
     def between(k):
-        @pl.when(k == 0)
-        def _():
-            accumulate(3)
-            accumulate(nz - 3)
-
         @pl.when(k == 1)
         def _():
             poll(nz // 2)
@@ -513,12 +510,13 @@
             down = spread(sq_sum, sq_d, d_send, d_recv, ddev)
     ortho_part(3)
     scale = lax.rsqrt(sum_of(sq_sum, sq_d, down) + NORM_EPS)
-    for copy in coming[0] + coming[1]:
-        copy.wait_recv()
-    for rows0 in range(0, trans_ref.shape[0], NB):
-        for j in range(n // NB):
-            value = trans_ref[rows0 : rows0 + NB, j * NB : (j + 1) * NB].astype(F32)
-            basis_ref[rows0 : rows0 + NB, j * NB : (j + 1) * NB] = (value * scale[j : j + 1, :]).astype(BF16)
+    for q in range(2):
+        for copy in coming[q]:
+            copy.wait_recv()
+        for rows0 in range(0, trans_ref.shape[0], NB):
+            for j in range(q * nblk // 2, (q + 1) * nblk // 2):
+                value = trans_ref[rows0 : rows0 + NB, j * NB : (j + 1) * NB].astype(F32)
+                basis_ref[rows0 : rows0 + NB, j * NB : (j + 1) * NB] = (value * scale[j : j + 1, :]).astype(BF16)
     for k in range(4):
         for s in range(2):
             mixed_copy(k, s)[0].wait_send()

time: 222 us -> 219 us (0.986)
  Pallas kernels: 219 us -> 216 us
    pallas_call x1, Pallas kernels: 138 us -> 135 us  [factor(): pl.pallas_call(factor_kernel, out_shape=[jax.ShapeDtypeStruct((prows * nt...]
where the time goes in v7:
time: 219 us; the launch traced here: 218 us
  Pallas kernels  216 us (99%)
    pallas_call x1, Pallas kernels, factor(): pl.pallas_call(factor_kernel, out_shape=[jax.ShapeDtypeStruct((prows * nt...  135 us
    pallas_call x1, Pallas kernels, project(): pl.pallas_call(project_kernel, out_shape=jax.ShapeDtypeStruct((rows, n),...  69.7 us
    pallas_call x1, Pallas kernels, outputs(): pl.pallas_call(functools.partial(output_kernel, scale_up), grid=(rows //...  11.6 us

profile of v7, /device:TPU:1, one launch (start us, length us, event | category | flops | bytes accessed | tf_op | source)
XLA Modules:
  0.0 218.4 jit_solution(12000697341596354401)
XLA Ops:
  0.6 69.7 %project.1.p_ref = f32[104,1024]{1,0:T(8,128)} custom-call(bf16[1664,1024]{1,0:T(8,128)(2,1)} %buf_ref.1, bf16[64,1024]{1,0:T(8,128)(2,1)} %bitcast.1), custom_call_target="tpu_custom_call" | custom-call | flops 20000000000 | bytes 16777216 | tf_op jit(solution)/shard_map/project/pallas_call | solution.py:709
  70.3 134.6 %factor.1 = (bf16[1664,1024]{1,0:T(8,128)(2,1)}, bf16[1024,1024]{1,0:T(8,128)(2,1)}, bf16[1024,1024]{1,0:T(8,128)(2,1)}) custom-call(f32[104,1024]{1,0:T(8,128)} %project.1.p_ref, bf16[1664,1024]{1,0:T(8,128)(2,1)} %buf_ref.1), custom_call_target="tpu_custom_call" | custom-call | flops 60000002048 | bytes 25165824 | tf_op jit(solution)/shard_map/factor/pallas_call | solution.py:550
  204.9 11.6 %outputs.1 = (bf16[1664,1024]{1,0:T(8,128)(2,1)}, bf16[1664,1024]{1,0:T(8,128)(2,1)}) custom-call(bf16[1664,1024]{1,0:T(8,128)(2,1)} %get-tuple-element.8.ortho_ref, bf16[1024,1024]{1,0:T(8,128)(2,1)} %get-tuple-element.9.trans_ref, bf16[1024,1024]{1,0:T(8,128)(2,1)} %get-tuple-element.10.basis_ref, bf16[1664,1024]{1,0:T(8,128)(2,1)} %buf_ref.1), custom_call_target="tpu_custom_call" | custom-call | flops 8000000000 | bytes 20971520 | tf_op jit(solution)/shard_map/outputs/pallas_call | solution.py:745
  216.5 1.1 constant_dynamic-slice_fusion
  217.6 0.8 copy.5
